TPU v7x, 128 devices: a whole 4x4x4 slice. The times are simulated.
128 devices in a mesh: section: 2 (over z_lo), batch: 64 (over y, x, z_hi, core).
Axes of the slice: x: 4, y: 4, z: 4 (z_hi: 2, z_lo: 2; z = z_hi * 2 + z_lo), core: 2. Of those that a mesh axis runs over, the one named last changes fastest.
Arguments:
- patch_io: bfloat16 [2, 2, 64, 64, 1024], P('section', None, 'batch'), may hold values from -6 to 6
- byte_states: bfloat16 [2, 64, 512, 1024], P(None, 'batch', 'section'), may hold values from -6 to 6
- patch_lengths: int32 [2, 64, 64], P(None, 'batch'), may hold values from 1 to 16, 512 in all within a row
- patch_live: int32 [2, 64, 64], P(None, 'batch'), may hold values 0 or 1
- attn_qkv: bfloat16 [2, 1024, 3072], P('section'), may hold values from -0.1875 to 0.1875
- attn_out: bfloat16 [2, 1024, 1024], P('section'), may hold values from -0.75 to 0.75
- gains: float32 [2, 2, 1024], P('section'), may hold values from 0.25 to 1.75
- ff_weights: bfloat16 [2816, 3, 1024], replicated, may hold values from -0.1875 to 0.1875
Outputs:
- patch_out: float32 [2, 2, 64, 64, 1024], P('section', None, 'batch')
- byte_grad: bfloat16 [2, 64, 512, 1024], P(None, 'batch', 'section')
- attn_qkv_grad: float32 [2, 1024, 3072], P('section')
- attn_out_grad: float32 [2, 1024, 1024], P('section')
- gains_grad: float32 [2, 2, 1024], P('section')
- ff_grad: float32 [2, 2816, 3, 1024], P('section', 'batch')
Inputs may be any that keep to these rules, and one draw needn't show every extreme that they name: `patch_lengths`: each row of 64 patch lengths sums to 512; the largest in a row is 16.
All inputs are finite; a program needn't handle non-finite values. No bound on the sum of `patch_live` on one device may be relied on, other than what follows from the above.
Results may differ from a plain program's by a relative error of at most 0.017.
Values may be sent and summed in bfloat16 or wider, within the bound.
No kernel may reach another device: no remote copies, remote signals or barrier semaphores. Data moves between devices by JAX's collectives and lax.ppermute only.
A program may use at most 384 MiB of HBM per device.

v0:
```python
import jax
import jax.numpy as jnp
from jax import lax
from jax.sharding import PartitionSpec as P

HEADS = 16
HD = 64


epsilon = 1e-05
neg_big = -1e30


def passed_along(value, axis, by):
    devices = lax.axis_size(axis)
    pairs = [(i, i + by) for i in range(devices) if 0 <= i + by < devices]
    return lax.ppermute(value, axis, pairs)


def rms_norm(rows, gain):
    mean_square = jnp.mean(rows * rows, axis=-1, keepdims=True)
    return rows * lax.rsqrt(mean_square + epsilon) * gain


def norm_back(rows, gain, upstream):
    outputs, pullback = jax.vjp(rms_norm, rows, gain)
    return pullback(upstream)


def dense(left, right):
    return jnp.dot(left, right, preferred_element_type=jnp.float32)


def dense_back(left, right):
    return jnp.einsum("sc,dc->sd", left, right, preferred_element_type=jnp.float32)


def on_section(flag, compute):
    return lax.cond(flag, compute, lambda: jax.tree.map(jnp.zeros_like, compute()))


def attend_forward(queries, keys, values, allowed, head_scale):
    raw = jnp.einsum("qhe,khe->hqk", queries, keys, preferred_element_type=jnp.float32)
    scores = jnp.where(allowed[None], raw * head_scale, neg_big)
    highest_score = jnp.max(scores, axis=-1, keepdims=True)
    exponent = jnp.exp(scores - highest_score)
    summed = jnp.sum(exponent, axis=-1, keepdims=True)
    weights = (exponent / summed).astype(jnp.bfloat16)
    mixed = jnp.einsum("hqk,khe->qhe", weights, values, preferred_element_type=jnp.float32)
    return (mixed.astype(jnp.bfloat16), highest_score + jnp.log(summed))


def attend_backward(queries, keys, values, allowed, log_summed, grad_mixed, head_scale):
    raw = jnp.einsum("qhe,khe->hqk", queries, keys, preferred_element_type=jnp.float32)
    scores = jnp.where(allowed[None], raw * head_scale, neg_big)
    weights = jnp.exp(scores - log_summed)
    weights_low = weights.astype(jnp.bfloat16)
    grad_values = jnp.einsum(
        "hqk,qhe->khe", weights_low, grad_mixed, preferred_element_type=jnp.float32
    ).astype(jnp.bfloat16)
    grad_weights = jnp.einsum(
        "qhe,khe->hqk", grad_mixed, values, preferred_element_type=jnp.float32
    )
    inner = jnp.sum(grad_weights * weights, axis=-1, keepdims=True)
    grad_scores = (weights * (grad_weights - inner)).astype(jnp.bfloat16)
    grad_queries = (
        jnp.einsum("hqk,khe->qhe", grad_scores, keys, preferred_element_type=jnp.float32)
        * head_scale
    ).astype(jnp.bfloat16)
    grad_keys = (
        jnp.einsum("hqk,qhe->khe", grad_scores, queries, preferred_element_type=jnp.float32)
        * head_scale
    ).astype(jnp.bfloat16)
    return (grad_queries, grad_keys, grad_values)


def shards(patch_io, byte_states, patch_lengths, patch_live, attn_qkv, attn_out, gains, ff_weights):
    section = lax.axis_index("section")
    first = section == 0
    second = section == 1
    head_scale = HD ** (-0.5)
    w_qkv = attn_qkv[0]
    w_out = attn_out[0]
    gain_pair = gains[0]
    own_rows = patch_io[0, :, 0]
    lower_bytes = byte_states[:, 0]
    upper_bytes = passed_along(lower_bytes, "section", -1)
    byte_rows = jnp.concatenate([lower_bytes, upper_bytes], axis=1)
    lengths = patch_lengths[:, 0]
    live = patch_live[:, 0]
    micro_count = own_rows.shape[0]
    seq = own_rows.shape[1]
    width = own_rows.shape[2]
    byte_count = byte_rows.shape[1]
    half_bytes = byte_count // 2

    def encoder_forward(patch_rows, bytes_in, allowed):
        patch_norm = rms_norm(patch_rows.astype(jnp.float32), gain_pair[0]).astype(jnp.bfloat16)
        byte_norm = rms_norm(bytes_in.astype(jnp.float32), gain_pair[1]).astype(jnp.bfloat16)
        queries = dense(patch_norm, w_qkv[:, :width]).astype(jnp.bfloat16)
        key_value = dense(byte_norm, w_qkv[:, width:]).astype(jnp.bfloat16)
        keys = key_value[:, :width].reshape(byte_count, HEADS, HD)
        values = key_value[:, width:].reshape(byte_count, HEADS, HD)
        mixed, log_summed = attend_forward(
            queries.reshape(seq, HEADS, HD), keys, values, allowed, head_scale
        )
        mixed = mixed.reshape(seq, width)
        hidden = patch_rows.astype(jnp.float32) + dense(mixed, w_out)
        return (
            hidden.astype(jnp.bfloat16),
            (patch_norm, byte_norm, queries, keys, values, mixed, log_summed),
        )

    def encoder_backward(grad_sent, patch_rows, bytes_in, allowed, kept):
        patch_norm, byte_norm, queries, keys, values, mixed, log_summed = kept
        grad_w_out = dense(mixed.T, grad_sent)
        grad_mixed = dense_back(grad_sent, w_out).astype(jnp.bfloat16).reshape(seq, HEADS, HD)
        grad_q, grad_k, grad_v = attend_backward(
            queries.reshape(seq, HEADS, HD),
            keys,
            values,
            allowed,
            log_summed,
            grad_mixed,
            head_scale,
        )
        grad_q = grad_q.reshape(seq, width)
        grad_kv = jnp.concatenate(
            [grad_k.reshape(byte_count, width), grad_v.reshape(byte_count, width)], axis=1
        )
        grad_w_qkv = jnp.concatenate(
            [dense(patch_norm.T, grad_q), dense(byte_norm.T, grad_kv)], axis=1
        )
        grad_patch_norm = dense_back(grad_q, w_qkv[:, :width])
        grad_byte_norm = dense_back(grad_kv, w_qkv[:, width:])
        grad_patch_rows, grad_gain_patch = norm_back(
            patch_rows.astype(jnp.float32), gain_pair[0], grad_patch_norm
        )
        grad_byte_rows, grad_gain_byte = norm_back(
            bytes_in.astype(jnp.float32), gain_pair[1], grad_byte_norm
        )
        patch_grad = grad_sent.astype(jnp.float32) + grad_patch_rows
        section_grads = (grad_w_qkv, grad_w_out, jnp.stack([grad_gain_patch, grad_gain_byte]))
        return (patch_grad, grad_byte_rows.astype(jnp.bfloat16), section_grads)

    def latent_layer(input_rows, cotangent, allowed):
        input_f = input_rows.astype(jnp.float32)
        input_norm = rms_norm(input_f, gain_pair[0]).astype(jnp.bfloat16)
        qkv = dense(input_norm, w_qkv).astype(jnp.bfloat16)
        queries = qkv[:, :width].reshape(seq, HEADS, HD)
        keys = qkv[:, width : 2 * width].reshape(seq, HEADS, HD)
        values = qkv[:, 2 * width :].reshape(seq, HEADS, HD)
        mixed, log_summed = attend_forward(queries, keys, values, allowed, head_scale)
        mixed = mixed.reshape(seq, width)
        after = input_f + dense(mixed, w_out)
        ffn_norm = rms_norm(after, gain_pair[1]).astype(jnp.bfloat16)
        gate_up = jnp.einsum(
            "sd,fkd->skf", ffn_norm, ff_weights[:, :2], preferred_element_type=jnp.float32
        )
        gate = gate_up[:, 0]
        upward = gate_up[:, 1]
        sigmoid_gate = jax.nn.sigmoid(gate)
        activated = gate * sigmoid_gate
        hidden = (activated * upward).astype(jnp.bfloat16)
        latents = after + dense(hidden, ff_weights[:, 2])
        grad_hidden = dense_back(cotangent, ff_weights[:, 2])
        grad_gate = grad_hidden * upward * (sigmoid_gate * (1.0 + gate * (1.0 - sigmoid_gate)))
        grad_upward = grad_hidden * activated
        grad_gate_up = jnp.stack([grad_gate, grad_upward], axis=1).astype(jnp.bfloat16)
        grad_ffn_norm = jnp.einsum(
            "skf,fkd->sd", grad_gate_up, ff_weights[:, :2], preferred_element_type=jnp.float32
        )
        grad_after_norm, grad_gain_ffn = norm_back(after, gain_pair[1], grad_ffn_norm)
        grad_after = cotangent.astype(jnp.float32) + grad_after_norm
        grad_branch = grad_after.astype(jnp.bfloat16)
        grad_w_out = dense(mixed.T, grad_branch)
        grad_mixed = dense_back(grad_branch, w_out).astype(jnp.bfloat16).reshape(seq, HEADS, HD)
        grad_q, grad_k, grad_v = attend_backward(
            queries, keys, values, allowed, log_summed, grad_mixed, head_scale
        )
        grad_qkv = jnp.concatenate(
            [grad_q.reshape(seq, width), grad_k.reshape(seq, width), grad_v.reshape(seq, width)],
            axis=1,
        )
        grad_w_qkv = dense(input_norm.T, grad_qkv)
        grad_input_norm = dense_back(grad_qkv, w_qkv)
        grad_input_rows, grad_gain_attn = norm_back(input_f, gain_pair[0], grad_input_norm)
        grad_input = (grad_after + grad_input_rows).astype(jnp.bfloat16)
        section_grads = (grad_w_qkv, grad_w_out, jnp.stack([grad_gain_attn, grad_gain_ffn]))
        return (latents, grad_input, section_grads, (ffn_norm, grad_gate_up, hidden))

    acc_qkv = jnp.zeros(w_qkv.shape, jnp.float32)
    acc_out = jnp.zeros(w_out.shape, jnp.float32)
    acc_gain = jnp.zeros(gain_pair.shape, jnp.float32)
    patch_results = []
    byte_results = []
    ffn_inputs = []
    ffn_grads = []
    ffn_hidden = []
    for index in range(micro_count):
        length_row = lengths[index]
        ends = jnp.cumsum(length_row)
        starts = ends - length_row
        spots = lax.iota(jnp.int32, byte_count)
        allowed_bytes = (spots[None, :] >= starts[:, None]) & (spots[None, :] < ends[:, None])
        places = lax.iota(jnp.int32, seq)
        diagonal = places[None, :] == places[:, None]
        allowed_causal = (places[None, :] <= places[:, None]) & (
            (live[index][None, :] == 1) | diagonal
        )
        sent, kept = on_section(
            first, lambda: encoder_forward(own_rows[index], byte_rows[index], allowed_bytes)
        )
        arrived = passed_along(sent, "section", 1)
        latents, grad_input, latent_grads, ffn_parts = on_section(
            second, lambda: latent_layer(arrived, own_rows[index], allowed_causal)
        )
        returned = passed_along(grad_input, "section", -1)
        patch_grad, byte_grad_rows, encoder_grads = on_section(
            first,
            lambda: encoder_backward(
                returned, own_rows[index], byte_rows[index], allowed_bytes, kept
            ),
        )
        upper_grad = passed_along(byte_grad_rows[half_bytes:], "section", 1)
        byte_results.append(jnp.where(first, byte_grad_rows[:half_bytes], upper_grad))
        patch_results.append(patch_grad + latents)
        acc_qkv = acc_qkv + encoder_grads[0] + latent_grads[0]
        acc_out = acc_out + encoder_grads[1] + latent_grads[1]
        acc_gain = acc_gain + encoder_grads[2] + latent_grads[2]
        ffn_inputs.append(ffn_parts[0])
        ffn_grads.append(ffn_parts[1])
        ffn_hidden.append(ffn_parts[2])
    total_qkv, total_out, total_gain = lax.psum((acc_qkv, acc_out, acc_gain), "batch")
    ffn_input_all = jnp.concatenate(ffn_inputs, axis=0)
    ffn_grad_all = jnp.concatenate(ffn_grads, axis=0)
    ffn_hidden_all = jnp.concatenate(ffn_hidden, axis=0)
    cotangent_all = own_rows.reshape(micro_count * seq, width)
    section_count = lax.axis_size("section")
    batch_count = lax.axis_size("batch")
    hidden_units = ff_weights.shape[0]
    half_share = hidden_units // (section_count * batch_count)

    def ffn_block(grad_source, hidden_source):
        grad_gate_up_w = jnp.einsum(
            "skf,sd->fkd", grad_source, ffn_input_all, preferred_element_type=jnp.float32
        )
        grad_down = jnp.einsum(
            "sf,sd->fd", hidden_source, cotangent_all, preferred_element_type=jnp.float32
        )
        return jnp.concatenate([grad_gate_up_w, grad_down[:, None]], axis=1)

    held = lax.psum_scatter(
        lax.cond(
            second,
            lambda: ffn_block(ffn_grad_all, ffn_hidden_all),
            lambda: jnp.zeros((2 * half_share * lax.axis_size("batch"), 3, width), jnp.float32),
        ),
        "batch",
        scatter_dimension=0,
        tiled=True,
    )
    ff_grad = jnp.where(second, held, jnp.zeros_like(held))
    patch_out = jnp.stack(patch_results)[None, :, None]
    byte_grad = jnp.stack(byte_results)[:, None]
    return (patch_out, byte_grad, total_qkv[None], total_out[None], total_gain[None], ff_grad[None])


def solution(mesh):
    in_specs = (
        P("section", None, "batch", None, None),
        P(None, "batch", "section", None),
        P(None, "batch", None),
        P(None, "batch", None),
        P("section", None, None),
        P("section", None, None),
        P("section", None, None),
        P(),
    )
    out_specs = (
        P("section", None, "batch", None, None),
        P(None, "batch", "section", None),
        P("section", None, None),
        P("section", None, None),
        P("section", None, None),
        P("section", "batch", None, None),
    )
    return jax.shard_map(shards, mesh=mesh, in_specs=in_specs, out_specs=out_specs, check_vma=False)
```

profile of v0, /device:TPU:7, one launch (start us, length us, event | category | flops | bytes accessed | tf_op | source)
XLA Modules:
  0.0 1517.3 jit_solution(16752396669345512898)
XLA Ops:
  11.3 22.1 %collective-permute-done = bf16[2,256,1024]{2,1,0:T(8,128)(2,1)S(1)} collective-permute-done((bf16[2,256,1024]{2,1,0:T(8,128)(2,1)}, bf16[2,256,1024]{2,1,0:T(8,128)(2,1)S(1)}, u32[]{:S(2)}, u32[]{:S(2)}) %collective-permute-start) | collective-permute-done | bytes 1048608 | tf_op jit(solution)/shard_map/ppermute | solution.py:17
  36.1 20.9 %conditional.10 = (bf16[64,1024]{1,0:T(8,128)(2,1)}, bf16[64,1024]{1,0:T(8,128)(2,1)S(1)}, bf16[512,1024]{1,0:T(8,128)(2,1)}, bf16[64,1024]{1,0:T(8,128)(2,1)}, ...) conditional(s32[]{:T(128)} %convert_element_type.307, () %tuple.70, ...), branch_computations={%region_28.29_spmd, %region_29.34_spmd} | conditional | flops 2561932800 | bytes 51676448 | solution.py:39
  37.7 2.1 fusion.126
  40.7 4.5 fusion.115
  45.3 1.5 fusion.236
  48.3 2.6 copy.161
  51.0 1.6 fusion.123
  53.2 1.6 convolution_convert_fusion.7
  54.8 2.2 fusion.125
  57.0 2.0 collective-permute-start.3
  59.0 24.8 %conditional.7 = (bf16[64,1024]{1,0:T(8,128)(2,1)S(1)}, bf16[64,1024]{1,0:T(8,128)(2,1)S(1)}, bf16[512,1024]{1,0:T(8,128)(2,1)}, bf16[64,1024]{1,0:T(8,128)(2,1)...) conditional(s32[]{:T(128)} %convert_element_type.307, () %tuple.64, ...), branch_computations={%region_1.2_spmd, %region_2.7_spmd} | conditional | flops 2561932800 | bytes 39093452 | solution.py:39
  59.3 1.5 fusion.5
  60.9 2.5 fusion.7
  64.2 2.1 fusion.13
  67.2 4.8 fusion.2
  72.0 1.5 fusion.230
  73.5 2.3 copy.137
  75.8 2.3 copy.136
  78.1 1.9 fusion.10
  80.7 1.6 convolution_convert_fusion
  87.7 15.5 %conditional.11 = (f32[64,1024]{1,0:T(8,128)S(1)}, bf16[64,1024]{1,0:T(8,128)(2,1)}, f32[1024,3072]{1,0:T(8,128)S(1)}, f32[1024,1024]{1,0:T(8,128)S(1)}, f32[2,1...) conditional(s32[]{:T(128)} %convert_element_type.308, () %tuple.69, ...), branch_computations={%region_34.35_spmd, %region_35.45_spmd} | conditional | flops 3887029248 | bytes 177872320 | solution.py:39
  91.9 1.6 broadcast.455
  104.5 3.2 copy-done.4
  109.0 16.1 %conditional.8 = (f32[64,1024]{1,0:T(8,128)}, bf16[64,1024]{1,0:T(8,128)(2,1)}, f32[1024,3072]{1,0:T(8,128)}, f32[1024,1024]{1,0:T(8,128)S(1)}, f32[2,1024]{1,0:...) conditional(s32[]{:T(128)} %convert_element_type.308, () %tuple.63, ...), branch_computations={%region_7.8_spmd, %region_8.18_spmd} | conditional | flops 3887029248 | bytes 179707328 | solution.py:39
  113.1 6.2 broadcast.419
  126.6 2.4 pad_maximum_fusion.22
  129.0 1.9 pad_maximum_fusion.23
  130.9 1.8 pad_maximum_fusion.24
  132.7 11.5 conditional.13
  132.7 11.5 broadcast.480
  144.2 33.8 %copy.196 = f32[2816,3,1024]{2,0,1:T(8,128)} copy(f32[2816,3,1024]{0,2,1:T(8,128)} %get-tuple-element.624) | data formatting | bytes 69206016 | tf_op jit(solution)/shard_map/cond | solution.py:254
  178.0 66.5 %conditional.12 = (f32[64,1024]{1,0:T(8,128)}, bf16[512,1024]{1,0:T(8,128)(2,1)}, f32[1024,1024]{1,0:T(8,128)}, f32[2,1024]{1,0:T(2,128)}, f32[1024,3072]{1,0:T(8,128)}) conditional(s32[]{:T(128)} %convert_element_type.307, () %tuple.68, (bf16[64,1024]{1,0:T(8,128)(2,1)}, pred[64,512]{1,0:T(8,128)(4,1)}, bf16[64,1024]{1,0:T(8,128)(2,1)S(1)}, ...), branch_computations={%region_45.46_spmd, %region_46.54_spmd} | conditional | flops 5195500032 | bytes 140955808 | solution.py:39
  182.2 2.3 convolution_convert_fusion.13
  184.5 1.7 copy.232
  187.1 1.6 subtract_exponential_fusion.7
  195.5 2.6 fusion.221
  198.8 1.7 fusion.217
  200.6 5.0 fusion.211
  207.7 3.7 fusion.251
  211.4 2.7 convolution_bitcast_fusion.3
  214.1 5.7 convolution_bitcast_fusion.2
  219.9 11.9 pad_maximum_fusion.15
  231.7 12.6 copy.224
  244.5 63.5 %conditional.9 = (f32[64,1024]{1,0:T(8,128)}, bf16[512,1024]{1,0:T(8,128)(2,1)S(1)}, f32[1024,1024]{1,0:T(8,128)}, f32[2,1024]{1,0:T(2,128)}, f32[1024,3072]{1,0:T(8,128)}) conditional(s32[]{:T(128)} %convert_element_type.307, () %tuple.62, (bf16[64,1024]{1,0:T(8,128)(2,1)}, pred[64,512]{1,0:T(8,128)(4,1)}, bf16[64,1024]{1,0:T(8,128)(2,1)}, ...), branch_computations={%region_18.19_spmd, %region_19.27_spmd} | conditional | flops 5195500032 | bytes 144774144 | solution.py:39
  245.8 1.5 fusion.95
  248.5 1.7 convolution_convert_fusion.6
  250.6 1.9 subtract_exponential_fusion.3
  254.7 1.7 fusion.102
  260.1 2.6 fusion.108
  263.3 1.7 fusion.104
  265.1 5.0 fusion.98
  271.3 3.7 fusion.250
  275.0 2.7 convolution_bitcast_fusion.1
  277.7 5.7 convolution_bitcast_fusion
  283.4 11.8 pad_maximum_fusion.5
  295.2 12.6 copy.220
  308.0 10.4 add_bitcast_fusion.3
  318.4 23.2 %add_bitcast_fusion.2 = f32[1,1024,3072]{2,1,0:T(8,128)} fusion(f32[1024,3072]{1,0:T(8,128)} %copy-done.4, f32[1024,3072]{1,0:T(8,128)} %get-tuple-element.447, f32[1024,3072]{1,0:T(8,128)} %get-tuple-element.445, f32[1024,3072]{1,0:T(8,128)} %get-tuple-element.283), kind=kLoop, calls=%fused_computation.360 | loop fusion | flops 9437184 | bytes 62914560 | tf_op jit(solution)/shard_map/broadcast_in_dim | solution.py:266
  343.5 1.9 slice.191
  345.4 8.9 collective-permute-start.6
  357.2 181.6 %psum.23 = f32[1,2,1024]{2,1,0:T(2,128)} all-reduce(f32[1,2,1024]{2,1,0:T(2,128)S(1)} %add_bitcast_fusion.6), channel_id=1, replica_groups=mesh['section'=2,'batch'=64] {'batch'}, use_global_device_ids=true, to_apply=%region_56.57 | all-reduce | flops 2048 | bytes 16384 | tf_op jit(solution)/shard_map/psum | solution.py:234
  543.9 950.4 %all-reduce.4.cloned.1.call-done = (f32[1,1024,3072]{2,1,0:T(8,128)}, f32[1,1024,1024]{2,1,0:T(8,128)}, f32[2816,3,1024]{2,0,1:T(8,128)}) async-done(((f32[1,1024,3072]{2,1,0:T(8,128)}, f32[1,1024,1024]{2,1,0:T(8,128)}, f32[2816,3,1024]{2,0,1:T(8,128)}), (f32[1,1024,3072]{2,1,0:T(8,128)}, f32[1,1024,1024]{2,1,0:T(8,128)}, f32[2816,3,1024]{2,0,1:T(8,128)})) %all-reduce.4.cloned.1.call-update) | async-done | bytes 51380240 | tf_op jit(solution)/shard_map/psum | solution.py:234
  1496.8 11.1 copy.342
  1508.0 2.0 copy.343
  (244 shorter events, 67.8 us)
Async XLA Ops:
  7.2 1487.1 %all-reduce.4.cloned.1.call-start = ((), (), s32[]{:S(2)}) async-start(), calls=%async_computation | async-start | bytes 102760448 | tf_op jit(solution)/shard_map/psum | solution.py:234
  7.2 26.1 %collective-permute-start = (bf16[2,256,1024]{2,1,0:T(8,128)(2,1)}, bf16[2,256,1024]{2,1,0:T(8,128)(2,1)S(1)}, u32[]{:S(2)}, u32[]{:S(2)}) collective-permute-start(bf16[2,256,1024]{2,1,0:T(8,128)(2,1)} %bitcast.454), channel_id=1, source_target_pairs={{64,0},{65,1},{66,2},{67,3},{68,4},{69,5},{70,6},{71,7},{72,8},{73... | collective-permute-start | bytes 3145736 | tf_op jit(solution)/shard_map/ppermute | solution.py:17
  11.3 23.5 %copy-start = (bf16[1,1024,1024]{2,1,0:T(8,128)(2,1)S(1)}, bf16[1,1024,1024]{2,1,0:T(8,128)(2,1)}, u32[]{:S(2)}) copy-start(bf16[1,1024,1024]{2,1,0:T(8,128)(2,1)} %param.27) | copy-start | bytes 6291460
  11.3 23.5 %copy-start.13 = (bf16[1,2,1,64,1024]{4,3,2,1,0:T(8,128)(2,1)S(1)}, bf16[1,2,1,64,1024]{4,3,2,1,0:T(8,128)(2,1)}, u32[]{:S(2)}) copy-start(bf16[1,2,1,64,1024]{4,3,2,1,0:T(8,128)(2,1)} %param.22) | copy-start | bytes 786436
  11.3 23.5 %copy-start.79 = (f32[1,2,1024]{2,1,0:T(2,128)S(1)}, f32[1,2,1024]{2,1,0:T(2,128)}, u32[]{:S(2)}) copy-start(f32[1,2,1024]{2,1,0:T(2,128)} %param.28) | copy-start | bytes 24580
  36.8 8.4 copy-start.65
  39.8 5.4 copy-start.41
  46.8 4.2 copy-start.70
  48.3 4.2 copy-start.9
  51.0 2.2 copy-start.22
  54.8 2.2 copy-start.10
  54.8 2.2 copy-start.72
  57.0 2.0 copy-start.83
  57.0 2.0 copy-start.73
  57.0 30.0 %collective-permute-start.3 = (bf16[64,1024]{1,0:T(8,128)(2,1)}, bf16[64,1024]{1,0:T(8,128)(2,1)}, u32[]{:S(2)}, u32[]{:S(2)}) collective-permute-start(bf16[64,1024]{1,0:T(8,128)(2,1)} %get-tuple-element.269), channel_id=1, source_target_pairs={{0,64},{1,65},{2,66},{3,67},{4,68},{5,69},{6,70},{7,71},{8,72},{9,... | collective-permute-start | bytes 393224 | tf_op jit(solution)/shard_map/ppermute | solution.py:17
  66.2 5.8 copy-start.43
  73.5 4.6 copy-start.68
  78.1 2.6 copy-start.24
  82.3 1.5 copy-start.76
  85.7 18.8 %collective-permute-start.1 = (bf16[64,1024]{1,0:T(8,128)(2,1)}, bf16[64,1024]{1,0:T(8,128)(2,1)S(1)}, u32[]{:S(2)}, u32[]{:S(2)}) collective-permute-start(bf16[64,1024]{1,0:T(8,128)(2,1)} %copy-done.80), channel_id=1, source_target_pairs={{0,64},{1,65},{2,66},{3,67},{4,68},{5,69},{6,70},{7,71},{8,72},{9,... | collective-permute-start | bytes 393224 | tf_op jit(solution)/shard_map/ppermute | solution.py:17
  103.2 4.5 copy-start.4
  103.2 5.8 copy-start.7
  103.2 74.8 %collective-permute-start.4 = (bf16[64,1024]{1,0:T(8,128)(2,1)}, bf16[64,1024]{1,0:T(8,128)(2,1)}, u32[]{:S(2)}, u32[]{:S(2)}) collective-permute-start(bf16[64,1024]{1,0:T(8,128)(2,1)} %get-tuple-element.270), channel_id=1, source_target_pairs={{64,0},{65,1},{66,2},{67,3},{68,4},{69,5},{70,6},{71,7},{72,8},{73... | collective-permute-start | bytes 393224 | tf_op jit(solution)/shard_map/ppermute | solution.py:17
  125.1 5.8 copy-start.8
  125.1 3.9 copy-start.40
  125.2 119.4 %collective-permute-start.2 = (bf16[64,1024]{1,0:T(8,128)(2,1)}, bf16[64,1024]{1,0:T(8,128)(2,1)}, u32[]{:S(2)}, u32[]{:S(2)}) collective-permute-start(bf16[64,1024]{1,0:T(8,128)(2,1)} %get-tuple-element.259), channel_id=1, source_target_pairs={{64,0},{65,1},{66,2},{67,3},{68,4},{69,5},{70,6},{71,7},{72,8},{73... | collective-permute-start | bytes 393224 | tf_op jit(solution)/shard_map/ppermute | solution.py:17
  126.6 4.3 copy-start.58
  144.2 33.8 %copy-start.42 = (bf16[64,1024]{1,0:T(8,128)(2,1)S(1)}, bf16[64,1024]{1,0:T(8,128)(2,1)}, u32[]{:S(2)}) copy-start(bf16[64,1024]{1,0:T(8,128)(2,1)} %get-tuple-element.271) | copy-start | bytes 393220
  144.2 33.8 %copy-start.84 = (f32[16,64,1]{1,0,2:T(8,128)S(1)}, f32[16,64,1]{1,0,2:T(8,128)}, u32[]{:S(2)}) copy-start(f32[16,64,1]{1,0,2:T(8,128)} %copy-done.83) | copy-start | bytes 12292
  187.1 1.7 copy-start.38
  188.7 1.4 copy-start.23
  191.9 3.5 copy-start.94
  194.2 6.3 copy-start.60
  194.2 6.3 copy-start.96
  195.5 5.0 copy-start.2
  195.5 5.0 copy-start.63
  195.5 5.0 copy-start.102
  200.5 5.6 copy-start.91
  207.7 3.7 copy-start.74
  211.4 2.7 copy-start.66
  244.5 5.8 copy-start.44
  245.8 4.7 copy-start.69
  245.8 4.7 copy-start.86
  247.4 5.1 copy-start.92
  252.5 1.4 copy-start.25
  256.4 3.6 copy-start.95
  256.4 3.6 copy-start.114
  258.7 6.4 copy-start.3
  258.7 6.4 copy-start.61
  258.7 6.4 copy-start.97
  258.7 6.4 copy-start.103
  260.1 5.0 copy-start.64
  265.1 5.6 copy-start.93
  271.3 3.7 copy-start.78
  275.0 2.7 copy-start.62
  275.0 2.7 copy-start.67
  341.7 14.8 copy-start.87
  341.7 14.8 copy-start.88
  341.7 14.8 copy-start.89
  341.7 197.1 %copy-start.57 = (f32[64,1024]{1,0:T(8,128)S(1)}, f32[64,1024]{1,0:T(8,128)}, u32[]{:S(2)}) copy-start(f32[64,1024]{1,0:T(8,128)} %copy-done.56) | copy-start | bytes 786436
  341.7 198.0 %copy-start.59 = (f32[64,1024]{1,0:T(8,128)S(1)}, f32[64,1024]{1,0:T(8,128)}, u32[]{:S(2)}) copy-start(f32[64,1024]{1,0:T(8,128)} %get-tuple-element.267) | copy-start | bytes 786436
  345.4 196.2 %collective-permute-start.6 = (bf16[256,1024]{1,0:T(8,128)(2,1)}, bf16[256,1024]{1,0:T(8,128)(2,1)S(1)}, u32[]{:S(2)}, u32[]{:S(2)}) collective-permute-start(bf16[256,1024]{1,0:T(8,128)(2,1)} %slice.191), channel_id=1, source_target_pairs={{0,64},{1,65},{2,66},{3,67},{4,68},{5,69},{6,70},{7,71},{8,72},{9,... | collective-permute-start | bytes 1572872 | tf_op jit(solution)/shard_map/ppermute | solution.py:17
  355.1 187.6 %collective-permute-start.5 = (bf16[256,1024]{1,0:T(8,128)(2,1)}, bf16[256,1024]{1,0:T(8,128)(2,1)S(1)}, u32[]{:S(2)}, u32[]{:S(2)}) collective-permute-start(bf16[256,1024]{1,0:T(8,128)(2,1)} %slice.189), channel_id=1, source_target_pairs={{0,64},{1,65},{2,66},{3,67},{4,68},{5,69},{6,70},{7,71},{8,72},{9,... | collective-permute-start | bytes 1572872 | tf_op jit(solution)/shard_map/ppermute | solution.py:17
  1496.8 11.1 copy-start.21
  (15 other events, 11.7 us)
Sparse Core Ops, SparseCore 0:
  341.8 1152.4 all-reduce.3
where the time goes:
time: 1530 us; the launch traced here: 1520 us
  waiting for transfers between devices  973 us (64%)
  blocking collectives  182 us (12%)
  local copies, waits for them, and re-layouts  139 us (9%)
  other arithmetic  94.1 us (6%)
  matrix products  79.7 us (5%)
  starting transfers between devices  17.5 us (1%)
  loops' own time  17 us (1%)
  between operations  15.5 us (1%)
    psum x1, waiting for transfers between devices, shards(): lax.psum((acc_qkv, acc_out, acc_gain), 'batch')  950 us
    psum x1, blocking collectives, shards(): lax.psum((acc_qkv, acc_out, acc_gain), 'batch')  182 us
    dot_general x12, matrix products, dense(): return jnp.dot(left, right, preferred_element_type=jnp.float32)  41.5 us
    cond x1, local copies, waits for them, and re-layouts, shards(): lax.cond(second, lambda: ffn_block(ffn_grad_all, ffn_hidden_all), lambda:...  33.8 us
  transfers between devices with their start and end apart: 8, of which 2 were waited for; matrix products, arithmetic and copies ran while one was open for 11% of the time, Pallas kernels for 0%

commit v1 on v0

v1 whole, which is shorter than its diff:
```python
import jax
import jax.numpy as jnp
from jax import lax
from jax.sharding import Mesh
from jax.sharding import PartitionSpec as P

HEADS = 16
HD = 64
SCALE = HD**-0.5
EPS = 1e-05
NEG = -1e30
BATCH = ("y", "x", "zh", "core")
BF = jnp.bfloat16
F32 = jnp.float32


def dot(left, right):
    return jnp.dot(left, right, preferred_element_type=F32)


def dot_t(left, right):
    return jnp.einsum("sc,dc->sd", left, right, preferred_element_type=F32)


def t_dot(left, right):
    return jnp.einsum("sa,sb->ab", left, right, preferred_element_type=F32)


def rms_norm(rows, gain):
    mean_square = jnp.mean(rows * rows, axis=-1, keepdims=True)
    return rows * lax.rsqrt(mean_square + EPS) * gain


def norm_back(rows, gain, upstream):
    outputs, pullback = jax.vjp(rms_norm, rows, gain)
    return pullback(upstream)


def shift(value, axis, by):
    size = lax.axis_size(axis)
    return lax.ppermute(value, axis, [(i, (i + by) % size) for i in range(size)])


def along(value, by):
    return lax.ppermute(value, "s", [(0, 1)] if by > 0 else [(1, 0)])


def pick(stack, index):
    return lax.dynamic_index_in_dim(stack, index, 0, keepdims=False)


def ring_scatter(stack, axis):
    me = lax.axis_index(axis)
    half = stack.shape[-1] // 2
    far = pick(stack, (me + 2) % 4)
    from_left = shift(far[..., :half], axis, 1)
    from_right = shift(far[..., half:], axis, -1)
    right = pick(stack, (me + 1) % 4)
    left = pick(stack, (me + 3) % 4)
    right = jnp.concatenate(
        [(right[..., :half].astype(F32) + from_left.astype(F32)).astype(BF), right[..., half:]], -1
    )
    left = jnp.concatenate(
        [left[..., :half], (left[..., half:].astype(F32) + from_right.astype(F32)).astype(BF)], -1
    )
    got_left = shift(right, axis, 1)
    got_right = shift(left, axis, -1)
    own = pick(stack, me)
    return (own.astype(F32) + got_left.astype(F32) + got_right.astype(F32)).astype(BF)


def ring_gather(block, axis):
    me = lax.axis_index(axis)
    half = block.shape[-1] // 2
    before = shift(block, axis, 1)
    after = shift(block, axis, -1)
    far_a = shift(before[..., :half], axis, 1)
    far_b = shift(after[..., half:], axis, -1)
    out = jnp.zeros((4,) + block.shape, block.dtype)
    for offset, piece in ((0, block), (1, after), (2, jnp.concatenate([far_a, far_b], -1)), (3, before)):
        out = lax.dynamic_update_index_in_dim(out, piece, (me + offset) % 4, 0)
    return out


def plane_scatter(blocks):
    half = blocks.shape[-1] // 2
    rows = blocks.shape[2]
    one = blocks[..., :half]
    two = jnp.swapaxes(blocks[..., half:], 0, 1)
    one = ring_scatter(one.reshape(4, 4 * rows, half), "y").reshape(4, rows, half)
    two = ring_scatter(two.reshape(4, 4 * rows, half), "x").reshape(4, rows, half)
    one = ring_scatter(one, "x")
    two = ring_scatter(two, "y")
    return jnp.concatenate([one, two], -1)


def plane_gather(block):
    half = block.shape[-1] // 2
    rows = block.shape[0]
    one = ring_gather(block[:, :half], "x")
    two = ring_gather(block[:, half:], "y")
    one = ring_gather(one.reshape(4 * rows, half), "y").reshape(4, 4, rows, half)
    two = ring_gather(two.reshape(4 * rows, half), "x").reshape(4, 4, rows, half)
    return jnp.concatenate([one, jnp.swapaxes(two, 0, 1)], -1)


def pair_scatter(block):
    me = lax.axis_index("zh")
    got = shift(pick(block, 1 - me), "zh", 1)
    return (pick(block, me).astype(F32) + got.astype(F32)).astype(BF)


def pair_gather(block, axis, dim):
    me = lax.axis_index(axis)
    got = shift(block, axis, 1)
    first = jnp.where(me == 0, block, got)
    second = jnp.where(me == 0, got, block)
    return jnp.concatenate([first, second], dim)


def small_sum(value):
    value = value + shift(value, "core", 1)
    value = value + shift(value, "zh", 1)
    for axis in ("x", "y"):
        value = value + shift(value, axis, 1)
        value = value + shift(value, axis, 2)
    return value


def heads(rows, count):
    return rows.reshape(2, count, HEADS, HD)


def attend_forward(queries, keys, values, allowed):
    raw = jnp.einsum("bqhe,bkhe->bhqk", queries, keys, preferred_element_type=F32)
    scores = jnp.where(allowed[:, None], raw * SCALE, NEG)
    highest = jnp.max(scores, axis=-1, keepdims=True)
    exponent = jnp.exp(scores - highest)
    summed = jnp.sum(exponent, axis=-1, keepdims=True)
    weights = (exponent / summed).astype(BF)
    mixed = jnp.einsum("bhqk,bkhe->bqhe", weights, values, preferred_element_type=F32)
    return mixed.astype(BF), highest + jnp.log(summed)


def attend_backward(queries, keys, values, allowed, log_summed, grad_mixed):
    raw = jnp.einsum("bqhe,bkhe->bhqk", queries, keys, preferred_element_type=F32)
    scores = jnp.where(allowed[:, None], raw * SCALE, NEG)
    weights = jnp.exp(scores - log_summed)
    grad_v = jnp.einsum(
        "bhqk,bqhe->bkhe", weights.astype(BF), grad_mixed, preferred_element_type=F32
    ).astype(BF)
    grad_w = jnp.einsum("bqhe,bkhe->bhqk", grad_mixed, values, preferred_element_type=F32)
    inner = jnp.sum(grad_w * weights, axis=-1, keepdims=True)
    grad_s = (weights * (grad_w - inner)).astype(BF)
    grad_q = (
        jnp.einsum("bhqk,bkhe->bqhe", grad_s, keys, preferred_element_type=F32) * SCALE
    ).astype(BF)
    grad_k = (
        jnp.einsum("bhqk,bqhe->bkhe", grad_s, queries, preferred_element_type=F32) * SCALE
    ).astype(BF)
    return grad_q, grad_k, grad_v


def on_section(flag, compute):
    return lax.cond(flag, compute, lambda: jax.tree.map(jnp.zeros_like, jax.eval_shape(compute)))


def shards(patch_io, byte_states, patch_lengths, patch_live, attn_qkv, attn_out, gains, ff_weights):
    section = lax.axis_index("s")
    core = lax.axis_index("core")
    first = section == 0
    second = section == 1
    w_qkv = attn_qkv[0]
    w_out = attn_out[0]
    gain_pair = gains[0]
    micro, seq, width = patch_io.shape[1], patch_io.shape[3], patch_io.shape[4]
    half_bytes = byte_states.shape[2]
    count = 2 * half_bytes
    rows = micro * seq
    own_rows = patch_io[0, :, 0].reshape(rows, width)
    own_f = own_rows.astype(F32)
    lower = byte_states[:, 0]
    upper = along(lower, -1)
    byte_rows = jnp.concatenate([lower, upper], axis=1).reshape(micro * count, width)
    lengths = patch_lengths[:, 0]
    live = patch_live[:, 0]
    ends = jnp.cumsum(lengths, axis=1)
    starts = ends - lengths
    spots = lax.iota(jnp.int32, count)
    allowed_bytes = (spots >= starts[..., None]) & (spots < ends[..., None])
    places = lax.iota(jnp.int32, seq)
    allowed_causal = (places[None, :] <= places[:, None])[None] & (
        (live[:, None, :] == 1) | (places[None, :] == places[:, None])[None]
    )

    def zeros(shape, dtype=BF):
        return jnp.zeros(shape, dtype)

    def encoder_forward():
        patch_norm = rms_norm(own_f, gain_pair[0]).astype(BF)
        byte_norm = rms_norm(byte_rows.astype(F32), gain_pair[1]).astype(BF)
        queries = dot(patch_norm, w_qkv[:, :width]).astype(BF)
        key_value = dot(byte_norm, w_qkv[:, width:]).astype(BF)
        keys = key_value[:, :width]
        values = key_value[:, width:]
        mixed, log_summed = attend_forward(
            heads(queries, seq), heads(keys, count), heads(values, count), allowed_bytes
        )
        mixed = mixed.reshape(rows, width)
        hidden = own_f + dot(mixed, w_out)
        return hidden.astype(BF), (patch_norm, byte_norm, queries, keys, values, mixed, log_summed)

    def encoder_backward(grad_sent, kept):
        patch_norm, byte_norm, queries, keys, values, mixed, log_summed = kept
        grad_mixed = dot_t(grad_sent, w_out).astype(BF)
        grad_q, grad_k, grad_v = attend_backward(
            heads(queries, seq),
            heads(keys, count),
            heads(values, count),
            allowed_bytes,
            log_summed,
            heads(grad_mixed, seq),
        )
        grad_q = grad_q.reshape(rows, width)
        grad_k = grad_k.reshape(micro * count, width)
        grad_v = grad_v.reshape(micro * count, width)
        grad_patch_rows, gain_patch = norm_back(own_f, gain_pair[0], dot_t(grad_q, w_qkv[:, :width]))
        grad_byte_norm = dot_t(grad_k, w_qkv[:, width : 2 * width]) + dot_t(grad_v, w_qkv[:, 2 * width :])
        grad_byte_rows, gain_byte = norm_back(byte_rows.astype(F32), gain_pair[1], grad_byte_norm)
        patch_grad = grad_sent.astype(F32) + grad_patch_rows
        return (
            patch_grad,
            grad_byte_rows.astype(BF),
            jnp.stack([gain_patch, gain_byte]),
            (grad_q, grad_k, grad_v),
        )

    def latent_layer(input_rows):
        cotangent = own_rows
        input_f = input_rows.astype(F32)
        input_norm = rms_norm(input_f, gain_pair[0]).astype(BF)
        qkv = dot(input_norm, w_qkv).astype(BF)
        queries = heads(qkv[:, :width], seq)
        keys = heads(qkv[:, width : 2 * width], seq)
        values = heads(qkv[:, 2 * width :], seq)
        mixed, log_summed = attend_forward(queries, keys, values, allowed_causal)
        mixed = mixed.reshape(rows, width)
        after = input_f + dot(mixed, w_out)
        ffn_norm = rms_norm(after, gain_pair[1]).astype(BF)
        gate = dot_t(ffn_norm, ff_weights[:, 0])
        upward = dot_t(ffn_norm, ff_weights[:, 1])
        sig = jax.nn.sigmoid(gate)
        activated = gate * sig
        hidden = (activated * upward).astype(BF)
        latents = after + dot(hidden, ff_weights[:, 2])
        grad_hidden = dot_t(cotangent, ff_weights[:, 2])
        grad_gate = (grad_hidden * upward * (sig * (1.0 + gate * (1.0 - sig)))).astype(BF)
        grad_upward = (grad_hidden * activated).astype(BF)
        grad_ffn_norm = dot(grad_gate, ff_weights[:, 0]) + dot(grad_upward, ff_weights[:, 1])
        grad_after_norm, gain_ffn = norm_back(after, gain_pair[1], grad_ffn_norm)
        grad_after = cotangent.astype(F32) + grad_after_norm
        grad_branch = grad_after.astype(BF)
        grad_mixed = dot_t(grad_branch, w_out).astype(BF)
        grad_q, grad_k, grad_v = attend_backward(
            queries, keys, values, allowed_causal, log_summed, heads(grad_mixed, seq)
        )
        grad_q, grad_k, grad_v = (g.reshape(rows, width) for g in (grad_q, grad_k, grad_v))
        grad_input_norm = dot_t(jnp.concatenate([grad_q, grad_k, grad_v], 1), w_qkv)
        grad_input_rows, gain_attn = norm_back(input_f, gain_pair[0], grad_input_norm)
        grad_input = (grad_after + grad_input_rows).astype(BF)
        return (
            latents,
            grad_input,
            jnp.stack([gain_attn, gain_ffn]),
            (input_norm, mixed, grad_branch, grad_q, grad_k, grad_v),
            (jnp.concatenate([grad_gate, grad_upward, hidden], 1), ffn_norm),
        )

    sent, kept = on_section(first, encoder_forward)
    arrived = along(sent, 1)
    latents, grad_input, latent_gain, attn_parts, ffn_parts = on_section(
        second, lambda: latent_layer(arrived)
    )
    returned = along(grad_input, -1)

    half = width // 2

    def mine(value):
        return lax.dynamic_slice_in_dim(value, core * half, half, value.ndim - 1)

    def other(value):
        return shift(lax.dynamic_slice_in_dim(value, (1 - core) * half, half, value.ndim - 1), "core", 1)

    def both(value):
        return jnp.concatenate([value, shift(value, "core", 1)], 0)

    def both_half(value):
        return jnp.concatenate([mine(value), other(value)], 0)

    acts = both(ffn_parts[0])
    norm_half = both_half(ffn_parts[1])
    cot_half = both_half(own_rows)
    units = ff_weights.shape[0]

    def ffn_grads():
        up_grad = t_dot(acts[:, : 2 * units], norm_half).astype(BF)
        down_grad = t_dot(acts[:, 2 * units :], cot_half).astype(BF)
        whole = jnp.concatenate([up_grad, down_grad], 0).reshape(3, 16, units // 16, half)
        return jnp.swapaxes(whole, 0, 1).reshape(4, 4, 3 * (units // 16), half)

    ff_blocks = on_section(second, ffn_grads)
    ff_sum = plane_scatter(ff_blocks).reshape(3, 2, units // 32, half)
    ff_sum = pair_scatter(jnp.swapaxes(ff_sum, 0, 1).reshape(2, 3 * (units // 32), half))
    ff_sum = jnp.swapaxes(ff_sum.reshape(3, 2, units // 64, half), 0, 1)
    ff_sum = pair_gather(pick(ff_sum, core), "core", -1) if False else jnp.where(
        core == 0,
        jnp.concatenate([ff_sum[0], shift(pick(ff_sum, 1 - core), "core", 1)], -1),
        jnp.concatenate([shift(pick(ff_sum, 1 - core), "core", 1), ff_sum[1]], -1),
    )
    ff_grad = jnp.where(second, jnp.swapaxes(ff_sum, 0, 1).astype(F32), 0.0)

    patch_grad, byte_grad_rows, encoder_gain, byte_parts = on_section(
        first, lambda: encoder_backward(returned, kept)
    )
    byte_grad_rows = byte_grad_rows.reshape(micro, count, width)
    upper_grad = along(byte_grad_rows[:, half_bytes:], 1)
    byte_grad = jnp.where(first, byte_grad_rows[:, :half_bytes], upper_grad)
    patch_out = jnp.where(first, patch_grad, latents)

    left_q = both(jnp.where(first, kept[0], attn_parts[0]))
    left_o = both(jnp.where(first, kept[5], attn_parts[1]))
    right_o = both_half(jnp.where(first, returned, attn_parts[2]))
    right_q = both_half(jnp.where(first, byte_parts[0], attn_parts[3]))
    left_b = both(kept[1])
    right_bk = both_half(byte_parts[1])
    right_bv = both_half(byte_parts[2])
    right_k = both_half(attn_parts[4])
    right_v = both_half(attn_parts[5])

    def byte_grads():
        return t_dot(left_b, right_bk).astype(BF), t_dot(left_b, right_bv).astype(BF)

    def patch_grads():
        return t_dot(left_q, right_k).astype(BF), t_dot(left_q, right_v).astype(BF)

    grads_k, grads_v = lax.cond(first, byte_grads, patch_grads)
    grads_q = t_dot(left_q, right_q).astype(BF)
    grads_o = t_dot(left_o, right_o).astype(BF)
    share = width // 16
    blocks = jnp.stack([g.reshape(16, share, half) for g in (grads_q, grads_k, grads_v, grads_o)], 1)
    reduced = plane_scatter(blocks.reshape(4, 4, 4 * share, half))
    reduced = pair_scatter(reduced.reshape(2, 2 * share, half))
    gathered = pair_gather(reduced, "zh", 0)
    gathered = plane_gather(gathered).reshape(16, 4, share, half)
    gathered = pair_gather(gathered, "core", -1)
    gathered = jnp.swapaxes(gathered, 0, 1).reshape(4, width, width).astype(F32)
    total_qkv = jnp.swapaxes(gathered[:3], 0, 1).reshape(width, 3 * width)
    total_out = gathered[3]
    total_gain = small_sum(jnp.where(first, encoder_gain, latent_gain))
    patch_out = patch_out.reshape(1, micro, 1, seq, width)
    return (
        patch_out,
        byte_grad[:, None],
        total_qkv[None],
        total_out[None],
        total_gain[None],
        ff_grad[None],
    )


def solution(mesh):
    fine = Mesh(mesh.devices.reshape(2, 4, 4, 2, 2), ("s",) + BATCH)
    in_specs = (
        P("s", None, BATCH, None, None),
        P(None, BATCH, "s", None),
        P(None, BATCH, None),
        P(None, BATCH, None),
        P("s", None, None),
        P("s", None, None),
        P("s", None, None),
        P(),
    )
    out_specs = (
        P("s", None, BATCH, None, None),
        P(None, BATCH, "s", None),
        P("s", None, None),
        P("s", None, None),
        P("s", None, None),
        P("s", BATCH, None, None),
    )
    return jax.shard_map(shards, mesh=fine, in_specs=in_specs, out_specs=out_specs, check_vma=False)
```

time: 1530 us -> 574 us (0.38)
  waiting for transfers between devices: 973 us -> 179 us
  blocking collectives: 182 us -> 0 us
  starting transfers between devices: 17.5 us -> 101 us
  other arithmetic: 94.1 us -> 68 us
  matrix products: 79.7 us -> 54.9 us
    psum x1 -> x0, waiting for transfers between devices: 950 us -> none  [shards(): lax.psum((acc_qkv, acc_out, acc_gain), 'batch')]
    psum x1 -> x0, blocking collectives: 182 us -> none  [shards(): lax.psum((acc_qkv, acc_out, acc_gain), 'batch')]
    ppermute x7 -> x75, waiting for transfers between devices: 22.1 us -> 179 us  [the longest x4 91.3 us: along(): return lax.ppermute(value, 's', [(0, 1)] if by > 0 else [(1, 0)])]
    ppermute x7 -> x75, starting transfers between devices: 17.5 us -> 101 us  [the longest x71 95.9 us: shift(): lax.ppermute(value, axis, [(i, (i + by) % size) for i in range(size)])]
    cond x91 -> x26, local copies, waits for them, and re-layouts: 62.2 us -> 13.5 us  [the longest x2 8.32 us: on_section(): lax.cond(flag, compute, lambda: jax.tree.map(jnp.zeros_like, jax.eval_sha...]
    reshape x6 -> x14, local copies, waits for them, and re-layouts: 6.23 us -> 40.6 us  [the longest x10 38.3 us: heads(): return rows.reshape(2, count, HEADS, HD)]
    broadcast_in_dim x4 -> x1, other arithmetic: 35.5 us -> 2.31 us  [shards(): byte_grad[:, None]]
    dot_general x32 -> x18, matrix products: 79.7 us -> 54.9 us  [the longest x4 15.2 us: dot_t(): return jnp.einsum('sc,dc->sd', left, right, preferred_element_type=F32)]
  transfers between devices with their start and end apart: 8 -> 75, of which waited for: 2 -> 31; matrix products, arithmetic and copies ran while one was open for 11% -> 27% of each run, Pallas kernels for 0% -> 0%
where the time goes in v1:
time: 574 us; the launch traced here: 567 us
  waiting for transfers between devices  179 us (31%)
  local copies, waits for them, and re-layouts  153 us (27%)
  starting transfers between devices  101 us (18%)
  other arithmetic  68 us (12%)
  matrix products  54.9 us (10%)
  loops' own time  8.36 us (1%)
    ppermute x71, starting transfers between devices, shift(): lax.ppermute(value, axis, [(i, (i + by) % size) for i in range(size)])  95.9 us
    ppermute x4, waiting for transfers between devices, along(): return lax.ppermute(value, 's', [(0, 1)] if by > 0 else [(1, 0)])  91.3 us
    ppermute x71, waiting for transfers between devices, shift(): lax.ppermute(value, axis, [(i, (i + by) % size) for i in range(size)])  87.5 us
    reshape x10, local copies, waits for them, and re-layouts, heads(): return rows.reshape(2, count, HEADS, HD)  38.3 us
    slice x2, local copies, waits for them, and re-layouts, shards(): total_qkv = jnp.swapaxes(gathered[:3], 0, 1).reshape(width, 3 * width)  24 us
    unnamed x53, local copies, waits for them, and re-layouts  19.1 us
    dot_general x4, matrix products, dot_t(): return jnp.einsum('sc,dc->sd', left, right, preferred_element_type=F32)  15.2 us
    another operation x16, local copies, waits for them, and re-layouts  12.8 us
  transfers between devices with their start and end apart: 75, of which 31 were waited for; matrix products, arithmetic and copies ran while one was open for 27% of the time, Pallas kernels for 0%

profile of v1, /device:TPU:7, one launch (start us, length us, event | category | flops | bytes accessed | tf_op | source)
XLA Modules:
  0.0 566.5 jit_solution(17490328356972184229)
XLA Ops:
  4.7 22.2 %collective-permute-done = bf16[2,256,1024]{2,1,0:T(8,128)(2,1)} collective-permute-done((bf16[2,256,1024]{2,1,0:T(8,128)(2,1)}, bf16[2,256,1024]{2,1,0:T(8,128)(2,1)}, u32[]{:S(2)}, u32[]{:S(2)}) %collective-permute-start) | collective-permute-done | bytes 1048608 | tf_op jit(solution)/shard_map/ppermute | solution.py:45
  28.6 45.6 %conditional.5 = (bf16[128,1024]{1,0:T(8,128)(2,1)}, bf16[128,1024]{1,0:T(8,128)(2,1)S(1)}, bf16[1024,1024]{1,0:T(8,128)(2,1)}, bf16[128,1024]{1,0:T(8,128)(2,1)...) conditional(s32[]{:T(128)} %convert_element_type.464, () %tuple.52, ...), branch_computations={%region_1.2_spmd, %region_2.7_spmd} | conditional | flops 5123472384 | bytes 72394968 | solution.py:165
  34.6 7.3 %fusion.9 = bf16[1024,2048]{1,0:T(8,128)(2,1)S(1)} fusion(bf16[1024,1024]{1,0:T(8,128)(2,1)} %fusion.2, bf16[1024,3072]{1,0:T(8,128)(2,1)} %get-tuple-element.95), kind=kOutput, calls=%fused_computation.14 | convolution fusion | flops 4297064448 | bytes 10485760 | tf_op jit(solution)/shard_map/cond/branch_1_fun/dot_general | solution.py:18
  44.4 6.6 %reshape.351 = bf16[2,512,16,64]{3,2,1,0:T(8,128)(2,1)} reshape(bf16[1024,1024]{1,0:T(8,128)(2,1)} %get-tuple-element.395) | data formatting | bytes 4194304 | tf_op jit(solution)/shard_map/cond/branch_1_fun/reshape | solution.py:131
  51.0 6.4 %reshape.352 = bf16[2,512,16,64]{3,2,1,0:T(8,128)(2,1)} reshape(bf16[1024,1024]{1,0:T(8,128)(2,1)} %get-tuple-element.394) | data formatting | bytes 4194304 | tf_op jit(solution)/shard_map/cond/branch_1_fun/reshape | solution.py:131
  57.4 4.9 fusion.12
  64.5 3.8 fusion.24
  70.8 2.9 fusion.30
  80.2 15.6 %conditional.6 = (f32[128,1024]{1,0:T(8,128)}, bf16[128,1024]{1,0:T(8,128)(2,1)}, f32[2,1024]{1,0:T(2,128)S(1)}, bf16[128,1024]{1,0:T(8,128)(2,1)}, bf16[128,102...) conditional(s32[]{:T(128)} %convert_element_type.465, () %tuple.51, ...), branch_computations={%region_7.8_spmd, %region_8.18_spmd} | conditional | flops 6701963264 | bytes 186680896 | solution.py:165
  108.5 68.3 %collective-permute-done.2 = bf16[128,1024]{1,0:T(8,128)(2,1)S(1)} collective-permute-done((bf16[128,1024]{1,0:T(8,128)(2,1)}, bf16[128,1024]{1,0:T(8,128)(2,1)S(1)}, u32[]{:S(2)}, u32[]{:S(2)}) %collective-permute-start.2) | collective-permute-done | bytes 262176 | tf_op jit(solution)/shard_map/ppermute | solution.py:45
  177.5 77.1 %conditional.7 = (f32[128,1024]{1,0:T(8,128)}, bf16[1024,1024]{1,0:T(8,128)(2,1)}, f32[2,1024]{1,0:T(2,128)S(1)}, bf16[128,1024]{1,0:T(8,128)(2,1)}, bf16[1024,1...) conditional(s32[]{:T(128)} %convert_element_type.464, () %tuple.50, (bf16[128,1024]{1,0:T(8,128)(2,1)S(1)}, ...), branch_computations={%region_18.19_spmd, %region_19.27_spmd} | conditional | flops 5543040000 | bytes 154744016 | solution.py:165
  185.0 6.4 %reshape.353 = bf16[2,512,16,64]{3,2,1,0:T(8,128)(2,1)} reshape(bf16[1024,1024]{1,0:T(8,128)(2,1)} %get-tuple-element.261) | data formatting | bytes 4194304 | tf_op jit(solution)/shard_map/cond/branch_1_fun/reshape | solution.py:131
  191.4 6.3 %reshape.354 = bf16[2,512,16,64]{3,2,1,0:T(8,128)(2,1)} reshape(bf16[1024,1024]{1,0:T(8,128)(2,1)} %get-tuple-element.258) | data formatting | bytes 4194304 | tf_op jit(solution)/shard_map/cond/branch_1_fun/reshape | solution.py:131
  197.7 5.4 copy.125
  206.1 3.4 multiply_reduce_fusion.5
  210.9 2.7 convert_bitcast_fusion
  220.5 3.8 copy.133
  229.9 4.4 copy.170
  234.3 4.8 fusion.104
  239.0 6.9 %fusion.98 = (f32[1024]{0:T(1024)S(1)}, f32[1024]{0:T(1024)S(1)}, f32[1024,1024]{1,0:T(8,128)}) fusion(bf16[1024,1024]{1,0:T(8,128)(2,1)S(1)} %get-tuple-element.119, f32[1024]{0:T(1024)S(1)} %fusion.123, f32[1024]{0:T(1024)S(1)} %bitcast.407, f32[1024,1024]{1,0:T(8,128)S(1)} %fusion.104, bf16[1024,1024]{0,1:T(8,128)(2,1)S(1)} %bitcast.354, ...), kind=kOutput, calls=%fused_computation.139 | convolution fusion | flops 2155870208 | bytes 14696448 | tf_op jit(solution)/shard_map/cond/branch_1_fun/sc,dc->sd/dot_general | solution.py:22
  246.0 3.9 copy.168
  249.9 4.5 fusion.94
  259.3 3.7 collective-permute-start.49
  268.7 2.8 collective-permute-done.51
  272.9 3.0 collective-permute-start.11
  275.9 3.2 collective-permute-start.5
  287.5 2.7 pad_maximum_fusion.5
  290.3 4.8 conditional.8
  309.6 3.4 collective-permute-start.16
  319.1 4.0 pad_maximum_fusion.4
  323.1 4.3 conditional.9
  323.1 4.3 broadcast.246
  327.4 3.8 fusion.172
  332.8 2.7 collective-permute-start.59
  341.3 6.5 %collective-permute-done.17 = bf16[256,128]{1,0:T(8,128)(2,1)S(1)} collective-permute-done((bf16[256,128]{1,0:T(8,128)(2,1)S(1)}, bf16[256,128]{1,0:T(8,128)(2,1)S(1)}, u32[]{:S(2)}, u32[]{:S(2)}) %collective-permute-start.17) | collective-permute-done | bytes 65568 | tf_op jit(solution)/shard_map/ppermute | solution.py:41
  347.9 5.4 collective-permute-done.19
  353.3 4.3 collective-permute-done.25
  357.8 2.9 collective-permute-done.27
  360.8 2.7 collective-permute-start.18
  370.6 2.9 collective-permute-start.29
  376.0 2.9 collective-permute-start.30
  387.1 3.2 collective-permute-done.39
  390.6 3.1 collective-permute-done.40
  404.3 6.2 %collective-permute-done.44 = bf16[1024,256]{1,0:T(8,128)(2,1)S(1)} collective-permute-done((bf16[1024,256]{1,0:T(8,128)(2,1)S(1)}, bf16[1024,256]{1,0:T(8,128)(2,1)S(1)}, u32[]{:S(2)}, u32[]{:S(2)}) %collective-permute-start.44) | collective-permute-done | bytes 524320 | tf_op jit(solution)/shard_map/ppermute | solution.py:41
  410.5 3.2 collective-permute-start.45
  413.7 7.3 %collective-permute-done.43 = bf16[1024,256]{1,0:T(8,128)(2,1)S(1)} collective-permute-done((bf16[1024,256]{1,0:T(8,128)(2,1)S(1)}, bf16[1024,256]{1,0:T(8,128)(2,1)S(1)}, u32[]{:S(2)}, u32[]{:S(2)}) %collective-permute-start.43) | collective-permute-done | bytes 524320 | tf_op jit(solution)/shard_map/ppermute | solution.py:41
  421.1 2.7 collective-permute-start.66
  425.4 5.2 collective-permute-done.46
  432.1 4.0 collective-permute-done.38
  440.5 17.1 %collective-permute-start.47 = (bf16[16,4,64,512]{3,2,1,0:T(8,128)(2,1)}, bf16[16,4,64,512]{3,2,1,0:T(8,128)(2,1)}, u32[]{:S(2)}, u32[]{:S(2)}) collective-permute-start(bf16[16,4,64,512]{3,2,1,0:T(8,128)(2,1)} %pad_maximum_fusion.7), channel_id=1, source_target_pairs={{0,1},{1,0},{2,3},{3,2},{4,5},{5,4},{6,7},{7,6},{8,9},{9,8},{10,11... | collective-permute-start | bytes 12582920 | tf_op jit(solution)/shard_map/ppermute | solution.py:41
  458.4 2.7 collective-permute-start.71
  461.2 3.5 collective-permute-done.69
  464.9 2.7 collective-permute-start.62
  468.4 4.8 collective-permute-done.64
  474.5 6.3 %collective-permute-done.70 = bf16[528,256]{1,0:T(8,128)(2,1)S(1)} collective-permute-done((bf16[528,256]{1,0:T(8,128)(2,1)S(1)}, bf16[528,256]{1,0:T(8,128)(2,1)S(1)}, u32[]{:S(2)}, u32[]{:S(2)}) %collective-permute-start.70) | collective-permute-done | bytes 270368 | tf_op jit(solution)/shard_map/ppermute | solution.py:41
  481.0 2.9 collective-permute-start.73
  488.1 4.0 collective-permute-start.74
  494.6 6.0 %broadcast_select_fusion.1 = (bf16[16,4,64,512]{3,2,1,0:T(8,128)(2,1)}, bf16[16,4,64,512]{3,2,1,0:T(8,128)(2,1)}) fusion(bf16[16,4,64,512]{3,2,1,0:T(8,128)(2,1)} %collective-permute-done.47, pred[]{:T(512)S(6)} %eq.77, bf16[16,4,64,256]{3,2,1,0:T(8,128)(2,1)S(1)} %bitcast.341, bf16[16,4,64,256]{3,2,1,0:T(8,128)(2,1)S(1)} %bitcast.343), kind=kLoop, calls=%fused_computation.194 | loop fusion | flops 12582912 | bytes 16777216 | tf_op jit(solution)/shard_map/jit(_where)/select_n | solution.py:116
  500.6 11.7 %convert_bitcast_fusion.1 = f32[4,16,64,1024]{3,2,0,1:T(8,128)} fusion(bf16[16,4,64,512]{3,2,1,0:T(8,128)(2,1)} %get-tuple-element.319, bf16[16,4,64,512]{3,2,1,0:T(8,128)(2,1)} %get-tuple-element.318), kind=kLoop, calls=%fused_computation.188 | loop fusion | flops 16777216 | bytes 25165824 | tf_op jit(solution)/shard_map/convert_element_type | solution.py:356
  512.3 4.8 slice.392
  517.1 12.1 %slice.391 = f32[3,16,64,1024]{3,2,0,1:T(8,128)} slice(f32[4,16,64,1024]{3,2,0,1:T(8,128)} %convert_bitcast_fusion.1), slice={[0:3], [0:16], [0:64], [0:1024]} | slice | bytes 25165824 | tf_op jit(solution)/shard_map/slice | solution.py:357
  529.2 11.9 %copy.148 = f32[3,16,64,1024]{3,2,1,0:T(8,128)} copy(f32[3,16,64,1024]{3,2,0,1:T(8,128)} %slice.391) | data formatting | bytes 25165824 | tf_op jit(solution)/shard_map/slice | solution.py:357
  541.1 12.6 %copy.149 = f32[1024,3,1024]{0,2,1:T(8,128)} copy(f32[1024,3,1024]{2,0,1:T(8,128)} %bitcast.330) | data formatting | bytes 25165824 | tf_op jit(solution)/shard_map/transpose | solution.py:357
  553.7 12.6 %copy.153 = f32[1,1024,3072]{2,1,0:T(8,128)} copy(f32[1,1024,3072]{1,2,0:T(8,128)} %bitcast.331) | data formatting | bytes 25165824
  (399 shorter events, 168.8 us)
Async XLA Ops:
  0.6 26.2 %collective-permute-start = (bf16[2,256,1024]{2,1,0:T(8,128)(2,1)}, bf16[2,256,1024]{2,1,0:T(8,128)(2,1)}, u32[]{:S(2)}, u32[]{:S(2)}) collective-permute-start(bf16[2,256,1024]{2,1,0:T(8,128)(2,1)} %bitcast.389), channel_id=1, source_target_pairs={{64,0},{65,1},{66,2},{67,3},{68,4},{69,5},{70,6},{71,7},{72,8},{73... | collective-permute-start | bytes 3145736 | tf_op jit(solution)/shard_map/ppermute | solution.py:45
  74.2 5.9 %collective-permute-start.1 = (bf16[128,1024]{1,0:T(8,128)(2,1)}, bf16[128,1024]{1,0:T(8,128)(2,1)S(1)}, u32[]{:S(2)}, u32[]{:S(2)}) collective-permute-start(bf16[128,1024]{1,0:T(8,128)(2,1)} %get-tuple-element.162), channel_id=1, source_target_pairs={{0,64},{1,65},{2,66},{3,67},{4,68},{5,69},{6,70},{7,71},{8,72},{9,... | collective-permute-start | bytes 786440 | tf_op jit(solution)/shard_map/ppermute | solution.py:45
  78.9 208.6 %collective-permute-start.8 = (bf16[1024,1024]{1,0:T(8,128)(2,1)}, bf16[1024,1024]{1,0:T(8,128)(2,1)}, u32[]{:S(2)}, u32[]{:S(2)}) collective-permute-start(bf16[1024,1024]{1,0:T(8,128)(2,1)} %get-tuple-element.177), channel_id=1, source_target_pairs={{0,1},{1,0},{2,3},{3,2},{4,5},{5,4},{6,7},{7,6},{8,9},{9,8},{10,11... | collective-permute-start | bytes 6291464 | tf_op jit(solution)/shard_map/ppermute | solution.py:41
  97.4 8.7 %collective-permute-start.6 = (bf16[128,512]{1,0:T(8,128)(2,1)S(1)}, bf16[128,512]{1,0:T(8,128)(2,1)S(1)}, u32[]{:S(2)}, u32[]{:S(2)}) collective-permute-start(bf16[128,512]{1,0:T(8,128)(2,1)S(1)} %get-tuple-element.375), channel_id=1, source_target_pairs={{0,1},{1,0},{2,3},{3,2},{4,5},{5,4},{6,7},{7,6},{8,9},{9,8},{10,11... | collective-permute-start | bytes 393224 | tf_op jit(solution)/shard_map/ppermute | solution.py:41
  100.7 6.3 %collective-permute-start.7 = (bf16[128,512]{1,0:T(8,128)(2,1)S(1)}, bf16[128,512]{1,0:T(8,128)(2,1)S(1)}, u32[]{:S(2)}, u32[]{:S(2)}) collective-permute-start(bf16[128,512]{1,0:T(8,128)(2,1)S(1)} %get-tuple-element.373), channel_id=1, source_target_pairs={{0,1},{1,0},{2,3},{3,2},{4,5},{5,4},{6,7},{7,6},{8,9},{9,8},{10,11... | collective-permute-start | bytes 393224 | tf_op jit(solution)/shard_map/ppermute | solution.py:41
  101.9 5.8 %collective-permute-start.55 = (bf16[128,512]{1,0:T(8,128)(2,1)S(1)}, bf16[128,512]{1,0:T(8,128)(2,1)S(1)}, u32[]{:S(2)}, u32[]{:S(2)}) collective-permute-start(bf16[128,512]{1,0:T(8,128)(2,1)S(1)} %get-tuple-element.367), channel_id=1, source_target_pairs={{0,1},{1,0},{2,3},{3,2},{4,5},{5,4},{6,7},{7,6},{8,9},{9,8},{10,11... | collective-permute-start | bytes 393224 | tf_op jit(solution)/shard_map/ppermute | solution.py:41
  102.3 74.5 %collective-permute-start.2 = (bf16[128,1024]{1,0:T(8,128)(2,1)}, bf16[128,1024]{1,0:T(8,128)(2,1)S(1)}, u32[]{:S(2)}, u32[]{:S(2)}) collective-permute-start(bf16[128,1024]{1,0:T(8,128)(2,1)} %get-tuple-element.163), channel_id=1, source_target_pairs={{64,0},{65,1},{66,2},{67,3},{68,4},{69,5},{70,6},{71,7},{72,8},{73... | collective-permute-start | bytes 786440 | tf_op jit(solution)/shard_map/ppermute | solution.py:45
  106.1 166.8 %collective-permute-start.4 = (bf16[128,1024]{1,0:T(8,128)(2,1)}, bf16[128,1024]{1,0:T(8,128)(2,1)}, u32[]{:S(2)}, u32[]{:S(2)}) collective-permute-start(bf16[128,1024]{1,0:T(8,128)(2,1)} %broadcast_select_fusion.5), channel_id=1, source_target_pairs={{0,1},{1,0},{2,3},{3,2},{4,5},{5,4},{6,7},{7,6},{8,9},{9,8},{10,11... | collective-permute-start | bytes 786440 | tf_op jit(solution)/shard_map/ppermute | solution.py:41
  258.7 28.5 %collective-permute-start.9 = (bf16[1024,512]{1,0:T(8,128)(2,1)S(1)}, bf16[1024,512]{1,0:T(8,128)(2,1)S(1)}, u32[]{:S(2)}, u32[]{:S(2)}) collective-permute-start(bf16[1024,512]{1,0:T(8,128)(2,1)S(1)} %get-tuple-element.337), channel_id=1, source_target_pairs={{0,1},{1,0},{2,3},{3,2},{4,5},{5,4},{6,7},{7,6},{8,9},{9,8},{10,11... | collective-permute-start | bytes 3145736 | tf_op jit(solution)/shard_map/ppermute | solution.py:41
  258.8 28.5 %collective-permute-start.10 = (bf16[1024,512]{1,0:T(8,128)(2,1)S(1)}, bf16[1024,512]{1,0:T(8,128)(2,1)S(1)}, u32[]{:S(2)}, u32[]{:S(2)}) collective-permute-start(bf16[1024,512]{1,0:T(8,128)(2,1)S(1)} %get-tuple-element.335), channel_id=1, source_target_pairs={{0,1},{1,0},{2,3},{3,2},{4,5},{5,4},{6,7},{7,6},{8,9},{9,8},{10,11... | collective-permute-start | bytes 3145736 | tf_op jit(solution)/shard_map/ppermute | solution.py:41
  259.3 5.6 collective-permute-start.49
  272.9 12.4 %collective-permute-start.11 = (bf16[128,1024]{1,0:T(8,128)(2,1)S(1)}, bf16[128,1024]{1,0:T(8,128)(2,1)S(1)}, u32[]{:S(2)}, u32[]{:S(2)}) collective-permute-start(bf16[128,1024]{1,0:T(8,128)(2,1)S(1)} %copy-done.49), channel_id=1, source_target_pairs={{0,1},{1,0},{2,3},{3,2},{4,5},{5,4},{6,7},{7,6},{8,9},{9,8},{10,11... | collective-permute-start | bytes 786440 | tf_op jit(solution)/shard_map/ppermute | solution.py:41
  275.9 6.7 %collective-permute-start.5 = (bf16[128,512]{1,0:T(8,128)(2,1)S(1)}, bf16[128,512]{1,0:T(8,128)(2,1)S(1)}, u32[]{:S(2)}, u32[]{:S(2)}) collective-permute-start(bf16[128,512]{1,0:T(8,128)(2,1)S(1)} %get-tuple-element.371), channel_id=1, source_target_pairs={{0,1},{1,0},{2,3},{3,2},{4,5},{5,4},{6,7},{7,6},{8,9},{9,8},{10,11... | collective-permute-start | bytes 393224 | tf_op jit(solution)/shard_map/ppermute | solution.py:41
  285.2 33.9 %collective-permute-start.54 = (bf16[128,8448]{1,0:T(8,128)(2,1)S(1)}, bf16[128,8448]{1,0:T(8,128)(2,1)}, u32[]{:S(2)}, u32[]{:S(2)}) collective-permute-start(bf16[128,8448]{1,0:T(8,128)(2,1)S(1)} %copy-done.8), channel_id=1, source_target_pairs={{0,1},{1,0},{2,3},{3,2},{4,5},{5,4},{6,7},{7,6},{8,9},{9,8},{10,11... | collective-permute-start | bytes 6488072 | tf_op jit(solution)/shard_map/ppermute | solution.py:41
  300.6 12.4 %collective-permute-start.13 = (bf16[1024,128]{1,0:T(8,128)(2,1)S(1)}, bf16[1024,128]{1,0:T(8,128)(2,1)S(1)}, u32[]{:S(2)}, u32[]{:S(2)}) collective-permute-start(bf16[1024,128]{1,0:T(8,128)(2,1)S(1)} %get-tuple-element.351), channel_id=1, source_target_pairs={{0,16},{16,32},{32,48},{48,0},{1,17},{17,33},{33,49},{49,1},{2,18}... | collective-permute-start | bytes 786440 | tf_op jit(solution)/shard_map/ppermute | solution.py:41
  300.7 8.0 %collective-permute-start.15 = (bf16[1024,128]{1,0:T(8,128)(2,1)S(1)}, bf16[1024,128]{1,0:T(8,128)(2,1)S(1)}, u32[]{:S(2)}, u32[]{:S(2)}) collective-permute-start(bf16[1024,128]{1,0:T(8,128)(2,1)S(1)} %get-tuple-element.352), channel_id=1, source_target_pairs={{0,48},{16,0},{32,16},{48,32},{1,49},{17,1},{33,17},{49,33},{2,50}... | collective-permute-start | bytes 786440 | tf_op jit(solution)/shard_map/ppermute | solution.py:41
  304.8 10.8 %collective-permute-start.21 = (bf16[1024,128]{1,0:T(8,128)(2,1)S(1)}, bf16[1024,128]{1,0:T(8,128)(2,1)S(1)}, u32[]{:S(2)}, u32[]{:S(2)}) collective-permute-start(bf16[1024,128]{1,0:T(8,128)(2,1)S(1)} %get-tuple-element.356), channel_id=1, source_target_pairs={{0,4},{4,8},{8,12},{12,0},{1,5},{5,9},{9,13},{13,1},{2,6},{6,10},{... | collective-permute-start | bytes 786440 | tf_op jit(solution)/shard_map/ppermute | solution.py:41
  306.4 8.2 %collective-permute-start.23 = (bf16[1024,128]{1,0:T(8,128)(2,1)S(1)}, bf16[1024,128]{1,0:T(8,128)(2,1)S(1)}, u32[]{:S(2)}, u32[]{:S(2)}) collective-permute-start(bf16[1024,128]{1,0:T(8,128)(2,1)S(1)} %get-tuple-element.357), channel_id=1, source_target_pairs={{0,12},{4,0},{8,4},{12,8},{1,13},{5,1},{9,5},{13,9},{2,14},{6,2},{... | collective-permute-start | bytes 786440 | tf_op jit(solution)/shard_map/ppermute | solution.py:41
  309.6 23.2 %collective-permute-start.16 = (bf16[1024,256]{1,0:T(8,128)(2,1)}, bf16[1024,256]{1,0:T(8,128)(2,1)S(1)}, u32[]{:S(2)}, u32[]{:S(2)}) collective-permute-start(bf16[1024,256]{1,0:T(8,128)(2,1)} %pad_maximum_fusion.18), channel_id=1, source_target_pairs={{0,48},{16,0},{32,16},{48,32},{1,49},{17,1},{33,17},{49,33},{2,50}... | collective-permute-start | bytes 1572872 | tf_op jit(solution)/shard_map/ppermute | solution.py:41
  314.0 21.5 %collective-permute-start.14 = (bf16[1024,256]{1,0:T(8,128)(2,1)}, bf16[1024,256]{1,0:T(8,128)(2,1)}, u32[]{:S(2)}, u32[]{:S(2)}) collective-permute-start(bf16[1024,256]{1,0:T(8,128)(2,1)} %pad_maximum_fusion.17), channel_id=1, source_target_pairs={{0,16},{16,32},{32,48},{48,0},{1,17},{17,33},{33,49},{49,1},{2,18}... | collective-permute-start | bytes 1572872 | tf_op jit(solution)/shard_map/ppermute | solution.py:41
  315.5 21.6 %collective-permute-start.24 = (bf16[1024,256]{1,0:T(8,128)(2,1)}, bf16[1024,256]{1,0:T(8,128)(2,1)S(1)}, u32[]{:S(2)}, u32[]{:S(2)}) collective-permute-start(bf16[1024,256]{1,0:T(8,128)(2,1)} %pad_maximum_fusion.20), channel_id=1, source_target_pairs={{0,12},{4,0},{8,4},{12,8},{1,13},{5,1},{9,5},{13,9},{2,14},{6,2},{... | collective-permute-start | bytes 1572872 | tf_op jit(solution)/shard_map/ppermute | solution.py:41
  316.5 22.1 %collective-permute-start.22 = (bf16[1024,256]{1,0:T(8,128)(2,1)}, bf16[1024,256]{1,0:T(8,128)(2,1)}, u32[]{:S(2)}, u32[]{:S(2)}) collective-permute-start(bf16[1024,256]{1,0:T(8,128)(2,1)} %pad_maximum_fusion.19), channel_id=1, source_target_pairs={{0,4},{4,8},{8,12},{12,0},{1,5},{5,9},{9,13},{13,1},{2,6},{6,10},{... | collective-permute-start | bytes 1572872 | tf_op jit(solution)/shard_map/ppermute | solution.py:41
  331.6 29.1 %collective-permute-start.57 = (bf16[2112,128]{1,0:T(8,128)(2,1)S(1)}, bf16[2112,128]{1,0:T(8,128)(2,1)S(1)}, u32[]{:S(2)}, u32[]{:S(2)}) collective-permute-start(bf16[2112,128]{1,0:T(8,128)(2,1)S(1)} %get-tuple-element.341), channel_id=1, source_target_pairs={{0,16},{16,32},{32,48},{48,0},{1,17},{17,33},{33,49},{49,1},{2,18}... | collective-permute-start | bytes 1622024 | tf_op jit(solution)/shard_map/ppermute | solution.py:41
  332.8 30.8 %collective-permute-start.59 = (bf16[2112,128]{1,0:T(8,128)(2,1)S(1)}, bf16[2112,128]{1,0:T(8,128)(2,1)S(1)}, u32[]{:S(2)}, u32[]{:S(2)}) collective-permute-start(bf16[2112,128]{1,0:T(8,128)(2,1)S(1)} %get-tuple-element.342), channel_id=1, source_target_pairs={{0,48},{16,0},{32,16},{48,32},{1,49},{17,1},{33,17},{49,33},{2,50}... | collective-permute-start | bytes 1622024 | tf_op jit(solution)/shard_map/ppermute | solution.py:41
  335.6 29.8 %collective-permute-start.65 = (bf16[2112,128]{1,0:T(8,128)(2,1)S(1)}, bf16[2112,128]{1,0:T(8,128)(2,1)S(1)}, u32[]{:S(2)}, u32[]{:S(2)}) collective-permute-start(bf16[2112,128]{1,0:T(8,128)(2,1)S(1)} %get-tuple-element.346), channel_id=1, source_target_pairs={{0,4},{4,8},{8,12},{12,0},{1,5},{5,9},{9,13},{13,1},{2,6},{6,10},{... | collective-permute-start | bytes 1622024 | tf_op jit(solution)/shard_map/ppermute | solution.py:41
  337.1 36.5 %collective-permute-start.67 = (bf16[2112,128]{1,0:T(8,128)(2,1)S(1)}, bf16[2112,128]{1,0:T(8,128)(2,1)S(1)}, u32[]{:S(2)}, u32[]{:S(2)}) collective-permute-start(bf16[2112,128]{1,0:T(8,128)(2,1)S(1)} %get-tuple-element.347), channel_id=1, source_target_pairs={{0,12},{4,0},{8,4},{12,8},{1,13},{5,1},{9,5},{13,9},{2,14},{6,2},{... | collective-permute-start | bytes 1622024 | tf_op jit(solution)/shard_map/ppermute | solution.py:41
  338.6 9.3 %collective-permute-start.17 = (bf16[256,128]{1,0:T(8,128)(2,1)S(1)}, bf16[256,128]{1,0:T(8,128)(2,1)S(1)}, u32[]{:S(2)}, u32[]{:S(2)}) collective-permute-start(bf16[256,128]{1,0:T(8,128)(2,1)S(1)} %get-tuple-element.378), channel_id=1, source_target_pairs={{0,4},{4,8},{8,12},{12,0},{1,5},{5,9},{9,13},{13,1},{2,6},{6,10},{... | collective-permute-start | bytes 196616 | tf_op jit(solution)/shard_map/ppermute | solution.py:41
  347.9 5.4 collective-permute-start.19
  360.7 5.2 collective-permute-start.20
  360.8 7.7 %collective-permute-start.18 = (bf16[256,256]{1,0:T(8,128)(2,1)S(1)}, bf16[256,256]{1,0:T(8,128)(2,1)S(1)}, u32[]{:S(2)}, u32[]{:S(2)}) collective-permute-start(bf16[256,256]{1,0:T(8,128)(2,1)S(1)} %pad_maximum_fusion.31), channel_id=1, source_target_pairs={{0,4},{4,8},{8,12},{12,0},{1,5},{5,9},{9,13},{13,1},{2,6},{6,10},{... | collective-permute-start | bytes 393224 | tf_op jit(solution)/shard_map/ppermute | solution.py:41
  365.4 5.1 collective-permute-start.26
  365.9 35.8 %collective-permute-start.60 = (bf16[2112,256]{1,0:T(8,128)(2,1)S(1)}, bf16[2112,256]{1,0:T(8,128)(2,1)S(1)}, u32[]{:S(2)}, u32[]{:S(2)}) collective-permute-start(bf16[2112,256]{1,0:T(8,128)(2,1)S(1)} %pad_maximum_fusion.12), channel_id=1, source_target_pairs={{0,48},{16,0},{32,16},{48,32},{1,49},{17,1},{33,17},{49,33},{2,50}... | collective-permute-start | bytes 3244040 | tf_op jit(solution)/shard_map/ppermute | solution.py:41
  368.5 35.2 %collective-permute-start.58 = (bf16[2112,256]{1,0:T(8,128)(2,1)S(1)}, bf16[2112,256]{1,0:T(8,128)(2,1)S(1)}, u32[]{:S(2)}, u32[]{:S(2)}) collective-permute-start(bf16[2112,256]{1,0:T(8,128)(2,1)S(1)} %pad_maximum_fusion.11), channel_id=1, source_target_pairs={{0,16},{16,32},{32,48},{48,0},{1,17},{17,33},{33,49},{49,1},{2,18}... | collective-permute-start | bytes 3244040 | tf_op jit(solution)/shard_map/ppermute | solution.py:41
  370.6 5.4 collective-permute-start.29
  376.0 5.4 collective-permute-start.30
  381.5 5.4 collective-permute-start.31
  381.6 5.3 collective-permute-start.32
  384.5 5.8 %collective-permute-start.39 = (bf16[256,256]{1,0:T(8,128)(2,1)S(1)}, bf16[256,256]{1,0:T(8,128)(2,1)S(1)}, u32[]{:S(2)}, u32[]{:S(2)}) collective-permute-start(bf16[256,256]{1,0:T(8,128)(2,1)S(1)} %get-tuple-element.285), channel_id=1, source_target_pairs={{0,48},{16,0},{32,16},{48,32},{1,49},{17,1},{33,17},{49,33},{2,50}... | collective-permute-start | bytes 393224 | tf_op jit(solution)/shard_map/ppermute | solution.py:41
  386.9 6.8 %collective-permute-start.40 = (bf16[256,256]{1,0:T(8,128)(2,1)S(1)}, bf16[256,256]{1,0:T(8,128)(2,1)S(1)}, u32[]{:S(2)}, u32[]{:S(2)}) collective-permute-start(bf16[256,256]{1,0:T(8,128)(2,1)S(1)} %get-tuple-element.285), channel_id=1, source_target_pairs={{0,16},{16,32},{32,48},{48,0},{1,17},{17,33},{33,49},{49,1},{2,18}... | collective-permute-start | bytes 393224 | tf_op jit(solution)/shard_map/ppermute | solution.py:41
  386.9 6.8 %collective-permute-start.34 = (bf16[256,128]{1,0:T(8,128)(2,1)S(1)}, bf16[256,128]{1,0:T(8,128)(2,1)S(1)}, u32[]{:S(2)}, u32[]{:S(2)}) collective-permute-start(bf16[256,128]{1,0:T(8,128)(2,1)S(1)} %slice.384), channel_id=1, source_target_pairs={{0,12},{4,0},{8,4},{12,8},{1,13},{5,1},{9,5},{13,9},{2,14},{6,2},{... | collective-permute-start | bytes 196616 | tf_op jit(solution)/shard_map/ppermute | solution.py:41
  390.3 5.1 collective-permute-start.33
  393.7 45.3 %collective-permute-start.68 = (bf16[2112,256]{1,0:T(8,128)(2,1)S(1)}, bf16[2112,256]{1,0:T(8,128)(2,1)S(1)}, u32[]{:S(2)}, u32[]{:S(2)}) collective-permute-start(bf16[2112,256]{1,0:T(8,128)(2,1)S(1)} %pad_maximum_fusion.14), channel_id=1, source_target_pairs={{0,12},{4,0},{8,4},{12,8},{1,13},{5,1},{9,5},{13,9},{2,14},{6,2},{... | collective-permute-start | bytes 3244040 | tf_op jit(solution)/shard_map/ppermute | solution.py:41
  397.2 26.7 %collective-permute-start.36 = (bf16[1024,256]{1,0:T(8,128)(2,1)S(1)}, bf16[1024,256]{1,0:T(8,128)(2,1)S(1)}, u32[]{:S(2)}, u32[]{:S(2)}) collective-permute-start(bf16[1024,256]{1,0:T(8,128)(2,1)S(1)} %bitcast.383), channel_id=1, source_target_pairs={{0,16},{16,32},{32,48},{48,0},{1,17},{17,33},{33,49},{49,1},{2,18}... | collective-permute-start | bytes 1572872 | tf_op jit(solution)/shard_map/ppermute | solution.py:41
  400.0 21.1 %collective-permute-start.35 = (bf16[1024,256]{1,0:T(8,128)(2,1)S(1)}, bf16[1024,256]{1,0:T(8,128)(2,1)S(1)}, u32[]{:S(2)}, u32[]{:S(2)}) collective-permute-start(bf16[1024,256]{1,0:T(8,128)(2,1)S(1)} %bitcast.384), channel_id=1, source_target_pairs={{0,48},{16,0},{32,16},{48,32},{1,49},{17,1},{33,17},{49,33},{2,50}... | collective-permute-start | bytes 1572872 | tf_op jit(solution)/shard_map/ppermute | solution.py:41
  401.6 8.8 %collective-permute-start.44 = (bf16[1024,256]{1,0:T(8,128)(2,1)S(1)}, bf16[1024,256]{1,0:T(8,128)(2,1)S(1)}, u32[]{:S(2)}, u32[]{:S(2)}) collective-permute-start(bf16[1024,256]{1,0:T(8,128)(2,1)S(1)} %bitcast.381), channel_id=1, source_target_pairs={{0,4},{4,8},{8,12},{12,0},{1,5},{5,9},{9,13},{13,1},{2,6},{6,10},{... | collective-permute-start | bytes 1572872 | tf_op jit(solution)/shard_map/ppermute | solution.py:41
  403.6 17.3 %collective-permute-start.43 = (bf16[1024,256]{1,0:T(8,128)(2,1)S(1)}, bf16[1024,256]{1,0:T(8,128)(2,1)S(1)}, u32[]{:S(2)}, u32[]{:S(2)}) collective-permute-start(bf16[1024,256]{1,0:T(8,128)(2,1)S(1)} %bitcast.382), channel_id=1, source_target_pairs={{0,12},{4,0},{8,4},{12,8},{1,13},{5,1},{9,5},{13,9},{2,14},{6,2},{... | collective-permute-start | bytes 1572872 | tf_op jit(solution)/shard_map/ppermute | solution.py:41
  410.5 14.8 %collective-permute-start.45 = (bf16[1024,128]{1,0:T(8,128)(2,1)S(1)}, bf16[1024,128]{1,0:T(8,128)(2,1)S(1)}, u32[]{:S(2)}, u32[]{:S(2)}) collective-permute-start(bf16[1024,128]{1,0:T(8,128)(2,1)S(1)} %slice.389), channel_id=1, source_target_pairs={{0,4},{4,8},{8,12},{12,0},{1,5},{5,9},{9,13},{13,1},{2,6},{6,10},{... | collective-permute-start | bytes 786440 | tf_op jit(solution)/shard_map/ppermute | solution.py:41
  421.0 9.7 %collective-permute-start.46 = (bf16[1024,128]{1,0:T(8,128)(2,1)S(1)}, bf16[1024,128]{1,0:T(8,128)(2,1)S(1)}, u32[]{:S(2)}, u32[]{:S(2)}) collective-permute-start(bf16[1024,128]{1,0:T(8,128)(2,1)S(1)} %slice.390), channel_id=1, source_target_pairs={{0,12},{4,0},{8,4},{12,8},{1,13},{5,1},{9,5},{13,9},{2,14},{6,2},{... | collective-permute-start | bytes 786440 | tf_op jit(solution)/shard_map/ppermute | solution.py:41
  421.1 19.4 %collective-permute-start.66 = (bf16[2112,256]{1,0:T(8,128)(2,1)S(1)}, bf16[2112,256]{1,0:T(8,128)(2,1)S(1)}, u32[]{:S(2)}, u32[]{:S(2)}) collective-permute-start(bf16[2112,256]{1,0:T(8,128)(2,1)S(1)} %pad_maximum_fusion.13), channel_id=1, source_target_pairs={{0,4},{4,8},{8,12},{12,0},{1,5},{5,9},{9,13},{13,1},{2,6},{6,10},{... | collective-permute-start | bytes 3244040 | tf_op jit(solution)/shard_map/ppermute | solution.py:41
  423.9 59.9 %collective-permute-start.3 = (bf16[2,256,1024]{2,1,0:T(8,128)(2,1)S(1)}, bf16[2,256,1024]{2,1,0:T(8,128)(2,1)S(1)}, u32[]{:S(2)}, u32[]{:S(2)}) collective-permute-start(bf16[2,256,1024]{2,1,0:T(8,128)(2,1)S(1)} %copy-done.36), channel_id=1, source_target_pairs={{0,64},{1,65},{2,66},{3,67},{4,68},{5,69},{6,70},{7,71},{8,72},{9,... | collective-permute-start | bytes 3145736 | tf_op jit(solution)/shard_map/ppermute | solution.py:45
  425.3 6.8 %collective-permute-start.37 = (bf16[1024,128]{1,0:T(8,128)(2,1)S(1)}, bf16[1024,128]{1,0:T(8,128)(2,1)S(1)}, u32[]{:S(2)}, u32[]{:S(2)}) collective-permute-start(bf16[1024,128]{1,0:T(8,128)(2,1)S(1)} %slice.385), channel_id=1, source_target_pairs={{0,16},{16,32},{32,48},{48,0},{1,17},{17,33},{33,49},{49,1},{2,18}... | collective-permute-start | bytes 786440 | tf_op jit(solution)/shard_map/ppermute | solution.py:41
  430.6 5.5 collective-permute-start.38
  432.1 35.6 %collective-permute-start.53 = (f32[2,1024]{1,0:T(2,128)S(1)}, f32[2,1024]{1,0:T(2,128)S(1)}, u32[]{:S(2)}, u32[]{:S(2)}) collective-permute-start(f32[2,1024]{1,0:T(2,128)S(1)} %add.495), channel_id=1, source_target_pairs={{0,32},{16,48},{32,0},{48,16},{1,33},{17,49},{33,1},{49,17},{2,34}... | collective-permute-start | bytes 24584 | tf_op jit(solution)/shard_map/ppermute | solution.py:41
  436.2 22.1 %collective-permute-start.61 = (bf16[528,128]{1,0:T(8,128)(2,1)S(1)}, bf16[528,128]{1,0:T(8,128)(2,1)S(1)}, u32[]{:S(2)}, u32[]{:S(2)}) collective-permute-start(bf16[528,128]{1,0:T(8,128)(2,1)S(1)} %get-tuple-element.360), channel_id=1, source_target_pairs={{0,4},{4,8},{8,12},{12,0},{1,5},{5,9},{9,13},{13,1},{2,6},{6,10},{... | collective-permute-start | bytes 405512 | tf_op jit(solution)/shard_map/ppermute | solution.py:41
  439.0 19.4 %collective-permute-start.63 = (bf16[528,128]{1,0:T(8,128)(2,1)S(1)}, bf16[528,128]{1,0:T(8,128)(2,1)S(1)}, u32[]{:S(2)}, u32[]{:S(2)}) collective-permute-start(bf16[528,128]{1,0:T(8,128)(2,1)S(1)} %get-tuple-element.361), channel_id=1, source_target_pairs={{0,12},{4,0},{8,4},{12,8},{1,13},{5,1},{9,5},{13,9},{2,14},{6,2},{... | collective-permute-start | bytes 405512 | tf_op jit(solution)/shard_map/ppermute | solution.py:41
  440.5 54.0 %collective-permute-start.47 = (bf16[16,4,64,512]{3,2,1,0:T(8,128)(2,1)}, bf16[16,4,64,512]{3,2,1,0:T(8,128)(2,1)}, u32[]{:S(2)}, u32[]{:S(2)}) collective-permute-start(bf16[16,4,64,512]{3,2,1,0:T(8,128)(2,1)} %pad_maximum_fusion.7), channel_id=1, source_target_pairs={{0,1},{1,0},{2,3},{3,2},{4,5},{5,4},{6,7},{7,6},{8,9},{9,8},{10,11... | collective-permute-start | bytes 12582920 | tf_op jit(solution)/shard_map/ppermute | solution.py:41
  458.3 6.5 %collective-permute-start.69 = (bf16[528,128]{1,0:T(8,128)(2,1)S(1)}, bf16[528,128]{1,0:T(8,128)(2,1)S(1)}, u32[]{:S(2)}, u32[]{:S(2)}) collective-permute-start(bf16[528,128]{1,0:T(8,128)(2,1)S(1)} %get-tuple-element.362), channel_id=1, source_target_pairs={{0,16},{16,32},{32,48},{48,0},{1,17},{17,33},{33,49},{49,1},{2,18}... | collective-permute-start | bytes 405512 | tf_op jit(solution)/shard_map/ppermute | solution.py:41
  458.4 6.4 %collective-permute-start.71 = (bf16[528,128]{1,0:T(8,128)(2,1)S(1)}, bf16[528,128]{1,0:T(8,128)(2,1)S(1)}, u32[]{:S(2)}, u32[]{:S(2)}) collective-permute-start(bf16[528,128]{1,0:T(8,128)(2,1)S(1)} %get-tuple-element.363), channel_id=1, source_target_pairs={{0,48},{16,0},{32,16},{48,32},{1,49},{17,1},{33,17},{49,33},{2,50}... | collective-permute-start | bytes 405512 | tf_op jit(solution)/shard_map/ppermute | solution.py:41
  464.8 8.4 %collective-permute-start.64 = (bf16[528,256]{1,0:T(8,128)(2,1)S(1)}, bf16[528,256]{1,0:T(8,128)(2,1)S(1)}, u32[]{:S(2)}, u32[]{:S(2)}) collective-permute-start(bf16[528,256]{1,0:T(8,128)(2,1)S(1)} %pad_maximum_fusion.22), channel_id=1, source_target_pairs={{0,12},{4,0},{8,4},{12,8},{1,13},{5,1},{9,5},{13,9},{2,14},{6,2},{... | collective-permute-start | bytes 811016 | tf_op jit(solution)/shard_map/ppermute | solution.py:41
  464.9 8.9 %collective-permute-start.62 = (bf16[528,256]{1,0:T(8,128)(2,1)S(1)}, bf16[528,256]{1,0:T(8,128)(2,1)S(1)}, u32[]{:S(2)}, u32[]{:S(2)}) collective-permute-start(bf16[528,256]{1,0:T(8,128)(2,1)S(1)} %pad_maximum_fusion.21), channel_id=1, source_target_pairs={{0,4},{4,8},{8,12},{12,0},{1,5},{5,9},{9,13},{13,1},{2,6},{6,10},{... | collective-permute-start | bytes 811016 | tf_op jit(solution)/shard_map/ppermute | solution.py:41
  467.8 6.7 %collective-permute-start.72 = (bf16[528,256]{1,0:T(8,128)(2,1)S(1)}, bf16[528,256]{1,0:T(8,128)(2,1)S(1)}, u32[]{:S(2)}, u32[]{:S(2)}) collective-permute-start(bf16[528,256]{1,0:T(8,128)(2,1)S(1)} %pad_maximum_fusion.24), channel_id=1, source_target_pairs={{0,48},{16,0},{32,16},{48,32},{1,49},{17,1},{33,17},{49,33},{2,50}... | collective-permute-start | bytes 811016 | tf_op jit(solution)/shard_map/ppermute | solution.py:41
  473.2 7.5 %collective-permute-start.70 = (bf16[528,256]{1,0:T(8,128)(2,1)S(1)}, bf16[528,256]{1,0:T(8,128)(2,1)S(1)}, u32[]{:S(2)}, u32[]{:S(2)}) collective-permute-start(bf16[528,256]{1,0:T(8,128)(2,1)S(1)} %pad_maximum_fusion.23), channel_id=1, source_target_pairs={{0,16},{16,32},{32,48},{48,0},{1,17},{17,33},{33,49},{49,1},{2,18}... | collective-permute-start | bytes 811016 | tf_op jit(solution)/shard_map/ppermute | solution.py:41
  481.0 6.9 %collective-permute-start.73 = (bf16[264,512]{1,0:T(8,128)(2,1)S(1)}, bf16[264,512]{1,0:T(8,128)(2,1)S(1)}, u32[]{:S(2)}, u32[]{:S(2)}) collective-permute-start(bf16[264,512]{1,0:T(8,128)(2,1)S(1)} %dynamic-slice_bitcast_fusion.12), channel_id=1, source_target_pairs={{0,2},{2,0},{1,3},{3,1},{4,6},{6,4},{5,7},{7,5},{8,10},{10,8},{9,1... | collective-permute-start | bytes 811016 | tf_op jit(solution)/shard_map/ppermute | solution.py:41
  488.1 5.0 collective-permute-start.74
  (47 other events, 672.1 us)

commit v2 on v1

v2 whole, which is shorter than its diff:
```python
import functools

import jax
import jax.numpy as jnp
from jax import lax
from jax.experimental import pallas as pl
from jax.experimental.pallas import tpu as pltpu
from jax.sharding import Mesh
from jax.sharding import PartitionSpec as P

HD = 64
SCALE = HD**-0.5
EPS = 1e-05
NEG = -1e30
BATCH = ("y", "x", "zh", "core")
BF = jnp.bfloat16
F32 = jnp.float32
D = 1024
HALF = 512
GROUP = 256
VMEM_BYTES = 60 * 1024 * 1024


def nn(a, b):
    return lax.dot_general(a, b, (((1,), (0,)), ((), ())), preferred_element_type=F32)


def nt(a, b):
    return lax.dot_general(a, b, (((1,), (1,)), ((), ())), preferred_element_type=F32)


def tn(a, b):
    return lax.dot_general(a, b, (((0,), (0,)), ((), ())), preferred_element_type=F32)


def inverse_rms(x):
    return lax.rsqrt(jnp.mean(x * x, axis=-1, keepdims=True) + EPS)


def norm_back(x, gain, up):
    r = inverse_rms(x)
    scaled = up * gain
    inner = jnp.mean(scaled * x, axis=-1, keepdims=True)
    return r * (scaled - x * (r * r * inner)), up * (x * r)


def stack_heads(rows):
    head = lax.broadcasted_iota(jnp.int32, rows.shape, 1) // HD
    return jnp.concatenate([jnp.where(head == h, rows, jnp.zeros_like(rows)) for h in range(4)], 0)


def unstack_heads(stacked):
    head = lax.broadcasted_iota(jnp.int32, (HD, GROUP), 1) // HD
    out = stacked[0:HD]
    for h in range(1, 4):
        out = jnp.where(head == h, stacked[h * HD : (h + 1) * HD], out)
    return out


def softmax_columns(scores):
    top = functools.reduce(jnp.maximum, [jnp.max(s, axis=0, keepdims=True) for s in scores])
    parts = [jnp.exp(s - top) for s in scores]
    inverse = 1.0 / sum(jnp.sum(p, axis=0, keepdims=True) for p in parts)
    return [(p * inverse).astype(BF) for p in parts]


def encode_lower(patch, low, w_qkv, gains, pn, q, bn, k, v):
    x = patch[...].astype(F32)
    normed = (x * inverse_rms(x) * gains[0:1]).astype(BF)
    pn[...] = normed
    q[...] = nn(normed, w_qkv[:, 0:D]).astype(BF)
    for i in range(2):
        at = pl.ds(i * 256, 256)
        b = low[at, :].astype(F32)
        normed = (b * inverse_rms(b) * gains[1:2]).astype(BF)
        bn[at, :] = normed
        k[at, :] = nn(normed, w_qkv[:, D : 2 * D]).astype(BF)
        v[at, :] = nn(normed, w_qkv[:, 2 * D :]).astype(BF)


def encode_rest(patch, up, w_qkv, w_out, gains, bounds, q, k_lo, v_lo, hb, o1, weights, bn, k, v):
    for i in range(2):
        at = pl.ds(i * 256, 256)
        b = up[at, :].astype(F32)
        normed = (b * inverse_rms(b) * gains[1:2]).astype(BF)
        bn[at, :] = normed
        k[at, :] = nn(normed, w_qkv[:, D : 2 * D]).astype(BF)
        v[at, :] = nn(normed, w_qkv[:, 2 * D :]).astype(BF)
    spot = lax.broadcasted_iota(jnp.int32, (256, GROUP), 0)
    for m in range(2):
        start = bounds[m, 0:1, :]
        end = bounds[m, 1:2, :]
        inside = [(spot + h * 256 >= start) & (spot + h * 256 < end) for h in range(2)]
        keys_at = pl.ds(m * 256, 256)
        for g in range(4):
            lanes = slice(g * GROUP, (g + 1) * GROUP)
            stacked = stack_heads(q[m * HD : (m + 1) * HD, lanes] * BF(SCALE))
            scores = [
                jnp.where(inside[h], nt(ref[keys_at, lanes], stacked), NEG)
                for h, ref in enumerate((k_lo, k))
            ]
            w = softmax_columns(scores)
            weights[m * 8 + g * 2] = w[0]
            weights[m * 8 + g * 2 + 1] = w[1]
            mixed = tn(w[0], v_lo[keys_at, lanes]) + tn(w[1], v[keys_at, lanes])
            o1[m * HD : (m + 1) * HD, lanes] = unstack_heads(mixed).astype(BF)
    hb[...] = (patch[...].astype(F32) + nn(o1[...], w_out[...])).astype(BF)


def latent_layer(
    ids, hb, cot, allowed, w_qkv, w_out, gains, w_ff,
    latents, dhb, gain_grad, xn, o2, acts, norms, grads_mine, grads_other,
    qkv, weights, ff_buf, acc_out, acc_norm, dqkv, sems,
):
    core = ids[0]
    units = w_ff.shape[1]
    step = ff_buf.shape[2]
    steps = units // step

    def fetch(i, slot):
        return pltpu.make_async_copy(
            w_ff.at[:, pl.ds(pl.multiple_of(i * step, 128), step), :], ff_buf.at[slot], sems.at[slot]
        )

    fetch(0, 0).start()
    x = hb[...].astype(F32)
    normed = (x * inverse_rms(x) * gains[0:1]).astype(BF)
    xn[...] = normed
    qkv[...] = nn(normed, w_qkv[...]).astype(BF)
    for m in range(2):
        rows = slice(m * HD, (m + 1) * HD)
        for g in range(4):
            lanes = slice(g * GROUP, (g + 1) * GROUP)
            k_lanes = slice(D + g * GROUP, D + (g + 1) * GROUP)
            v_lanes = slice(2 * D + g * GROUP, 2 * D + (g + 1) * GROUP)
            stacked = stack_heads(qkv[rows, lanes] * BF(SCALE))
            scores = jnp.where(allowed[m] > 0.5, nt(qkv[rows, k_lanes], stacked), NEG)
            (w,) = softmax_columns([scores])
            weights[m * 4 + g] = w
            o2[rows, lanes] = unstack_heads(tn(w, qkv[rows, v_lanes])).astype(BF)
    after = x + nn(o2[...], w_out[...])
    yn = (after * inverse_rms(after) * gains[1:2]).astype(BF)
    c = cot[...]
    for h in range(2):
        lanes = slice(h * HALF, (h + 1) * HALF)
        norms[h, 0:128, :] = yn[:, lanes]
        norms[h, 128:256, :] = c[:, lanes]
    acc_out[...] = after
    acc_norm[...] = jnp.zeros_like(acc_norm)

    def ff_step(i, carry):
        slot = lax.rem(i, 2)

        @pl.when(i + 1 < steps)
        def _():
            fetch(i + 1, 1 - slot).start()

        fetch(i, slot).wait()
        w_gate, w_up, w_down = ff_buf.at[slot, 0], ff_buf.at[slot, 1], ff_buf.at[slot, 2]
        gate = nt(yn, w_gate[...])
        upward = nt(yn, w_up[...])
        du = nt(c, w_down[...])
        sig = 1.0 / (1.0 + jnp.exp(-gate))
        active = gate * sig
        hidden = (active * upward).astype(BF)
        d_gate = (du * upward * (sig * (1.0 + gate * (1.0 - sig)))).astype(BF)
        d_up = (du * active).astype(BF)
        at = pl.ds(pl.multiple_of(i * step, 128), step)
        acts[0, :, at] = d_gate
        acts[1, :, at] = d_up
        acts[2, :, at] = hidden
        acc_out[...] += nn(hidden, w_down[...])
        acc_norm[...] += nn(d_gate, w_gate[...]) + nn(d_up, w_up[...])
        return carry

    lax.fori_loop(0, steps, ff_step, 0)
    latents[...] = acc_out[...]
    back, gain_rows = norm_back(after, gains[1:2], acc_norm[...])
    gain_grad[1:2, :] = jnp.sum(gain_rows, axis=0, keepdims=True)
    d_after = c.astype(F32) + back
    da = d_after.astype(BF)
    d_mixed = nt(da, w_out[...]).astype(BF)
    for m in range(2):
        rows = slice(m * HD, (m + 1) * HD)
        for g in range(4):
            lanes = slice(g * GROUP, (g + 1) * GROUP)
            k_lanes = slice(D + g * GROUP, D + (g + 1) * GROUP)
            v_lanes = slice(2 * D + g * GROUP, 2 * D + (g + 1) * GROUP)
            q_stacked = stack_heads(qkv[rows, lanes] * BF(SCALE))
            o_stacked = stack_heads(d_mixed[rows, lanes])
            w_low = weights[m * 4 + g]
            w = w_low.astype(F32)
            dw = nt(qkv[rows, v_lanes], o_stacked)
            inner = jnp.sum(dw * w, axis=0, keepdims=True)
            ds = (w * (dw - inner)).astype(BF)
            dqkv[rows, lanes] = (unstack_heads(tn(ds, qkv[rows, k_lanes])) * SCALE).astype(BF)
            dqkv[rows, k_lanes] = nn(ds, q_stacked).astype(BF)
            dqkv[rows, v_lanes] = nn(w_low, o_stacked).astype(BF)
    d_normed = nt(dqkv[...], w_qkv[...])
    back, gain_rows = norm_back(x, gains[0:1], d_normed)
    gain_grad[0:1, :] = jnp.sum(gain_rows, axis=0, keepdims=True)
    dhb[...] = (d_after + back).astype(BF)
    for h in range(2):
        lanes = slice(h * HALF, (h + 1) * HALF)

        def put(target):
            target[0:128, :] = dqkv[:, h * HALF : (h + 1) * HALF]
            target[128:256, :] = da[:, lanes]
            target[256:384, :] = dqkv[:, D + h * HALF : D + (h + 1) * HALF]
            target[384:512, :] = dqkv[:, 2 * D + h * HALF : 2 * D + (h + 1) * HALF]

        @pl.when(core == h)
        def _():
            put(grads_mine)

        @pl.when(core != h)
        def _():
            put(grads_other)


def encoder_attention_back(
    ids, dhb, w_out, q, k_lo, k_up, v_lo, v_up, weights, grads_mine, grads_other
):
    core = ids[0]
    d_mixed = nt(dhb[...], w_out[...]).astype(BF)
    for g in range(4):
        lanes = slice(g * GROUP, (g + 1) * GROUP)
        out_lanes = slice((g % 2) * GROUP, (g % 2 + 1) * GROUP)

        def put(at, value, g=g, out_lanes=out_lanes):
            @pl.when(core == g // 2)
            def _():
                grads_mine[at, out_lanes] = value

            @pl.when(core != g // 2)
            def _():
                grads_other[at, out_lanes] = value

        put(slice(128, 256), dhb[:, lanes])
        for m in range(2):
            rows = slice(m * HD, (m + 1) * HD)
            keys_at = pl.ds(m * 256, 256)
            q_stacked = stack_heads(q[rows, lanes] * BF(SCALE))
            o_stacked = stack_heads(d_mixed[rows, lanes])
            low = [weights[m * 8 + g * 2 + h] for h in range(2)]
            w = [piece.astype(F32) for piece in low]
            dw = [nt(ref[keys_at, lanes], o_stacked) for ref in (v_lo, v_up)]
            inner = sum(jnp.sum(a * b, axis=0, keepdims=True) for a, b in zip(dw, w))
            ds = [(b * (a - inner)).astype(BF) for a, b in zip(dw, w)]
            dq = tn(ds[0], k_lo[keys_at, lanes]) + tn(ds[1], k_up[keys_at, lanes])
            put(rows, (unstack_heads(dq) * SCALE).astype(BF))
            for h in range(2):
                base = h * HALF + m * 256
                put(slice(256 + base, 512 + base), nn(ds[h], q_stacked).astype(BF))
                put(slice(1280 + base, 1536 + base), nn(low[h], o_stacked).astype(BF))


def encoder_input_back(
    ids, dhb, patch, low, up, w_qkv, gains, grads_mine, grads_other, patch_grad, low_grad, up_grad, gain_grad
):
    core = ids[0]
    parts = ((grads_mine, core), (grads_other, 1 - core))

    def columns(block, which):
        return pl.ds(pl.multiple_of(block * D + which * HALF, HALF), HALF)

    up_norm = sum(nt(ref[0:128, :], w_qkv[:, columns(0, which)]) for ref, which in parts)
    x = patch[...].astype(F32)
    back, gain_rows = norm_back(x, gains[0:1], up_norm)
    gain_grad[0:1, :] = jnp.sum(gain_rows, axis=0, keepdims=True)
    patch_grad[...] = dhb[...].astype(F32) + back
    total = jnp.zeros((1, D), F32)
    for h, (source, target) in enumerate(((low, low_grad), (up, up_grad))):
        for m in range(2):
            base = h * HALF + m * 256
            d_norm = sum(
                nt(ref[256 + base : 512 + base, :], w_qkv[:, columns(1, which)])
                + nt(ref[1280 + base : 1536 + base, :], w_qkv[:, columns(2, which)])
                for ref, which in parts
            )
            at = slice(m * 256, (m + 1) * 256)
            back, gain_rows = norm_back(source[at, :].astype(F32), gains[1:2], d_norm)
            total = total + jnp.sum(gain_rows, axis=0, keepdims=True)
            target[at, :] = back.astype(BF)
    gain_grad[1:2, :] = total


def turn_encoder(pn, o1, bn_lo, bn_up, left, left_bytes):
    left[0:D, :] = pn[...].T
    left[D : 2 * D, :] = o1[...].T
    left_bytes[:, 0:HALF] = bn_lo[...].T
    left_bytes[:, HALF : 2 * HALF] = bn_up[...].T


def turn_latent(xn, o2, left):
    left[0:D, :] = xn[...].T
    left[D : 2 * D, :] = o2[...].T


def turn_acts(acts, out):
    units = acts.shape[2]
    for j in range(3):
        out[j * units : (j + 1) * units, :] = acts[j].T


def encoder_weights(ids, left, left_far, bytes_near, bytes_far, near, far, *blocks):
    u = ids[1]
    for k in range(4):
        at = pl.ds(pl.multiple_of(lax.rem(u + k, 4) * 256, 256), 256)
        low_at = pl.ds(pl.multiple_of(lax.rem(u + k, 4) * 256 + D, 256), 256)
        blocks[k][0] = (nn(left[at, :], near[0:128, :]) + nn(left_far[at, :], far[0:128, :])).astype(BF)
        blocks[k][3] = (
            nn(left[low_at, :], near[128:256, :]) + nn(left_far[low_at, :], far[128:256, :])
        ).astype(BF)
        blocks[k][1] = (
            nn(bytes_near[at, :], near[256:1280, :]) + nn(bytes_far[at, :], far[256:1280, :])
        ).astype(BF)
        blocks[k][2] = (
            nn(bytes_near[at, :], near[1280:2304, :]) + nn(bytes_far[at, :], far[1280:2304, :])
        ).astype(BF)


def latent_weights(ids, left, left_far, near, far, *blocks):
    u = ids[1]
    for k in range(4):
        at = pl.ds(pl.multiple_of(lax.rem(u + k, 4) * 256, 256), 256)
        low_at = pl.ds(pl.multiple_of(lax.rem(u + k, 4) * 256 + D, 256), 256)
        for block, (source, first) in enumerate(((at, 0), (at, 256), (at, 384), (low_at, 128))):
            rows = slice(first, first + 128)
            blocks[k][block] = (
                nn(left[source, :], near[rows, :]) + nn(left_far[source, :], far[rows, :])
            ).astype(BF)


def ff_weights_grad(ids, acts, acts_far, near, far, *blocks):
    core, u = ids[0], ids[1]
    units = acts.shape[0] // 3
    share = units // 16
    for k in range(4):
        there = lax.rem(u + k, 4)
        for v in range(4):
            chunk = jnp.where(core == 0, there * 4 + v, v * 4 + there)
            for j in range(3):
                at = pl.ds(pl.multiple_of(j * units + chunk * share, 16), share)
                rows = slice(0, 128) if j < 2 else slice(128, 256)
                blocks[k][v, j * share : (j + 1) * share, :] = (
                    nn(acts[at, :], near[rows, :]) + nn(acts_far[at, :], far[rows, :])
                ).astype(BF)


def sum_four(own, a, b, c):
    return own.astype(F32) + a.astype(F32) + b.astype(F32) + c.astype(F32)


def attn_sum_first(ids, own, a, b, c, *outs):
    v = ids[2]
    for k in range(4):
        at = pl.ds(pl.multiple_of(lax.rem(v + k, 4) * HD, HD), HD)
        for block in range(4):
            outs[k][block] = sum_four(
                own[block, at, :], a[block, at, :], b[block, at, :], c[block, at, :]
            ).astype(BF)


def attn_sum_second(ids, own, a, b, c, mine, other):
    zh = ids[3]
    for target, which in ((mine, zh), (other, 1 - zh)):
        at = pl.ds(pl.multiple_of(which * 32, 32), 32)
        for block in range(4):
            target[block] = sum_four(
                own[block, at, :], a[block, at, :], b[block, at, :], c[block, at, :]
            ).astype(BF)


def ff_sum_first(ids, own, a, b, c, *outs):
    v = ids[2]
    for k in range(4):
        at = lax.rem(v + k, 4)
        outs[k][...] = sum_four(own[at], a[at], b[at], c[at]).astype(BF)


def ff_sum_second(own, a, b, c, out):
    out[...] = sum_four(own[...], a[...], b[...], c[...]).astype(BF)


def final_attn(ids, *refs):
    pieces, (qkv, out) = refs[:8], refs[8:]
    step = pl.program_id(0)
    for side in range(2):
        core = ids[0] if side == 0 else 1 - ids[0]
        u = ids[1] if side == 0 else ids[2]
        v = ids[2] if side == 0 else ids[1]
        zh = ids[3]
        for k in range(4):
            piece = pieces[side * 4 + k]

            @pl.when(lax.rem(u + k, 4) == step)
            def _(piece=piece, v=v, core=core, zh=zh):
                for j in range(4):
                    for z in range(2):
                        row = lax.rem(v + j, 4) * HD + jnp.where(zh == 0, z, 1 - z) * 32
                        at = pl.ds(pl.multiple_of(row, 32), 32)
                        for block in range(4):
                            value = piece[j, z, block].astype(F32)
                            first = core * HALF + (block * D if block < 3 else 0)
                            lanes = pl.ds(pl.multiple_of(first, HALF), HALF)
                            if block < 3:
                                qkv[at, lanes] = value
                            else:
                                out[at, lanes] = value


SMEM = pltpu.MemorySpace.SMEM
VMEM = pltpu.MemorySpace.VMEM


def call(kernel, args, outs, scratch=(), spaces=None, flops=0, moved=0):
    spaces = spaces or {}
    specs = [pl.BlockSpec(memory_space=spaces.get(i, VMEM)) for i in range(len(args))]
    return pl.pallas_call(
        kernel,
        out_shape=[jax.ShapeDtypeStruct(s, t) for s, t in outs],
        in_specs=specs,
        out_specs=[pl.BlockSpec(memory_space=VMEM) for _ in outs],
        scratch_shapes=list(scratch),
        compiler_params=pltpu.CompilerParams(vmem_limit_bytes=VMEM_BYTES),
        cost_estimate=pl.CostEstimate(flops=flops, bytes_accessed=moved, transcendentals=0),
    )(*args)


def nothing(outs):
    def kernel(*refs):
        pass

    return pl.pallas_call(
        kernel,
        out_shape=[jax.ShapeDtypeStruct(s, t) for s, t in outs],
        out_specs=[pl.BlockSpec(memory_space=pl.ANY) for _ in outs],
    )()


def on_section(flag, kernel, args, outs, **rest):
    return lax.cond(
        flag, lambda: call(kernel, args, outs, **rest), lambda: nothing(outs)
    )


def shift(value, axis, by):
    size = lax.axis_size(axis)
    return lax.ppermute(value, axis, [(i, (i + by) % size) for i in range(size)])


def along(value, by):
    return lax.ppermute(value, "s", [(0, 1)] if by > 0 else [(1, 0)])


def plane_shift(value, which, by, sections=(0, 1)):
    pairs = []
    for s in sections:
        for y in range(4):
            for x in range(4):
                for core in range(2):
                    ty, tx = ((y + by) % 4, x) if core == which else (y, (x + by) % 4)
                    pairs.append((((s * 4 + y) * 4 + x) * 2 + core, ((s * 4 + ty) * 4 + tx) * 2 + core))
    return lax.ppermute(value, ("s", "y", "x", "core"), pairs)


def exchange(blocks, which, sections=(0, 1)):
    return [plane_shift(blocks[k], which, k, sections) for k in (1, 2, 3)]


def collect(block, which):
    return [block] + [plane_shift(block, which, -k) for k in (1, 2, 3)]


def small_sum(value):
    value = value + shift(value, "core", 1)
    value = value + shift(value, "zh", 1)
    for axis in ("x", "y"):
        value = value + shift(value, axis, 1)
        value = value + shift(value, axis, 2)
    return value


def shards(patch_io, byte_states, patch_lengths, patch_live, attn_qkv, attn_out, gains, ff_weights):
    section = lax.axis_index("s")
    core = lax.axis_index("core")
    zh = lax.axis_index("zh")
    y, x = lax.axis_index("y"), lax.axis_index("x")
    first = section == 0
    second = section == 1
    ids = jnp.stack([core, jnp.where(core == 0, y, x), jnp.where(core == 0, x, y), zh]).astype(jnp.int32)
    w_qkv = attn_qkv[0]
    w_out = attn_out[0]
    gain_pair = gains[0]
    micro, seq = patch_io.shape[1], patch_io.shape[3]
    half_bytes = byte_states.shape[2]
    units = ff_weights.shape[0]
    rows = micro * seq
    own_rows = patch_io.reshape(rows, D)
    lower = byte_states.reshape(micro * half_bytes, D)
    upper = along(lower, -1)
    w_ff = jnp.swapaxes(ff_weights, 0, 1)
    lengths = patch_lengths[:, 0]
    live = patch_live[:, 0]
    ends = jnp.cumsum(lengths, axis=1)
    bounds = jnp.tile(jnp.stack([ends - lengths, ends], 1), (1, 1, 4))
    places = lax.iota(jnp.int32, seq)
    causal = places[:, None] <= places[None, :]
    diagonal = places[:, None] == places[None, :]
    allowed = causal[None] & ((live[:, :, None] == 1) | diagonal[None])
    allowed = jnp.tile(allowed.astype(F32), (1, 1, 4))

    wide = ((rows, D), BF)
    tall = ((micro * half_bytes, D), BF)
    pn, q, bn_lo, k_lo, v_lo = on_section(
        first, encode_lower, (own_rows, lower, w_qkv, gain_pair), [wide, wide, tall, tall, tall]
    )
    hb, o1, weights, bn_up, k_up, v_up = on_section(
        first,
        encode_rest,
        (own_rows, upper, w_qkv, w_out, gain_pair, bounds, q, k_lo, v_lo),
        [wide, wide, ((16, 256, GROUP), BF), tall, tall, tall],
    )
    arrived = along(hb, 1)
    grads_short = ((512, HALF), BF)
    step = 256
    latents, dhb, latent_gain, xn, o2, acts, norms, lat_mine, lat_other = on_section(
        second,
        latent_layer,
        (ids, arrived, own_rows, allowed, w_qkv, w_out, gain_pair, w_ff),
        [
            ((rows, D), F32), wide, ((2, D), F32), wide, wide,
            ((3, rows, units), BF), ((2, 256, HALF), BF), grads_short, grads_short,
        ],
        spaces={0: SMEM, 7: pl.ANY},
        scratch=[
            pltpu.VMEM((rows, 3 * D), BF),
            pltpu.VMEM((8, HD, GROUP), BF),
            pltpu.VMEM((2, 3, step, D), BF),
            pltpu.VMEM((rows, D), F32),
            pltpu.VMEM((rows, D), F32),
            pltpu.VMEM((rows, 3 * D), BF),
            pltpu.SemaphoreType.DMA((2,)),
        ],
    )
    returned = along(dhb, -1)

    left, left_bytes = lax.cond(
        first,
        lambda: call(turn_encoder, (pn, o1, bn_lo, bn_up), [((2 * D, rows), BF), ((D, 2 * HALF), BF)]),
        lambda: call(turn_latent, (xn, o2), [((2 * D, rows), BF)]) + nothing([((D, 2 * HALF), BF)]),
    )
    left_far = shift(left, "core", 1)
    bytes_far = shift(left_bytes, "core", 1)

    (acts_t,) = on_section(second, turn_acts, (acts,), [((3 * units, rows), BF)])
    acts_far = shift(acts_t, "core", 1)
    norms_near = lax.dynamic_index_in_dim(norms, core, 0, keepdims=False)
    norms_far = shift(lax.dynamic_index_in_dim(norms, 1 - core, 0, keepdims=False), "core", 1)
    share = units // 16
    ff_block = ((4, 3 * share, HALF), BF)
    ff_blocks = on_section(
        second, ff_weights_grad, (ids, acts_t, acts_far, norms_near, norms_far), [ff_block] * 4, spaces={0: SMEM}
    )
    ff_line = ((3 * share, HALF), BF)
    ff_got = exchange(ff_blocks, 0, (1,))
    ff_blocks = on_section(second, ff_sum_first, (ids, ff_blocks[0], *ff_got), [ff_line] * 4, spaces={0: SMEM})
    ff_got = exchange(ff_blocks, 1, (1,))
    (ff_sum,) = on_section(second, ff_sum_second, (ff_blocks[0], *ff_got), [ff_line])
    ff_sum = ff_sum.reshape(3, 2, share // 2, HALF)
    ff_own = lax.dynamic_index_in_dim(ff_sum, zh, 1, keepdims=False)
    ff_far = shift(lax.dynamic_index_in_dim(ff_sum, 1 - zh, 1, keepdims=False), "zh", 1)
    ff_sum = (ff_own.astype(F32) + ff_far.astype(F32)).astype(BF).reshape(3, 2, share // 4, HALF)
    ff_own = lax.dynamic_index_in_dim(ff_sum, core, 1, keepdims=False)
    ff_far = shift(lax.dynamic_index_in_dim(ff_sum, 1 - core, 1, keepdims=False), "core", 1)
    ff_pair = jnp.stack([jnp.where(core == 0, ff_own, ff_far), jnp.where(core == 0, ff_far, ff_own)], 2)
    ff_grad = jnp.swapaxes(ff_pair.reshape(3, share // 4, D), 0, 1).astype(F32)
    ff_grad = jnp.where(second, ff_grad, 0.0)

    grads_long = ((2304, HALF), BF)
    enc_mine, enc_other = on_section(
        first,
        encoder_attention_back,
        (ids, returned, w_out, q, k_lo, k_up, v_lo, v_up, weights),
        [grads_long, grads_long],
        spaces={0: SMEM},
    )
    enc_far = shift(enc_other, "core", 1)
    lat_far = shift(lat_other, "core", 1)
    attn_block = ((4, 256, HALF), BF)
    blocks = lax.cond(
        first,
        lambda: call(
            encoder_weights,
            (ids, left, left_far, left_bytes, bytes_far, enc_mine, enc_far),
            [attn_block] * 4,
            spaces={0: SMEM},
        ),
        lambda: call(
            latent_weights, (ids, left, left_far, lat_mine, lat_far), [attn_block] * 4, spaces={0: SMEM}
        ),
    )
    patch_grad, low_grad, up_grad, encoder_gain = on_section(
        first,
        encoder_input_back,
        (ids, returned, own_rows, lower, upper, w_qkv, gain_pair, enc_mine, enc_other),
        [((rows, D), F32), tall, tall, ((2, D), F32)],
        spaces={0: SMEM},
    )
    up_arrived = along(up_grad, 1)
    byte_grad = jnp.where(first, low_grad, up_arrived)
    patch_out = jnp.where(first, patch_grad, latents)

    got = exchange(blocks, 0)
    blocks = call(attn_sum_first, (ids, blocks[0], *got), [((4, HD, HALF), BF)] * 4, spaces={0: SMEM})
    got = exchange(blocks, 1)
    mine, other = call(attn_sum_second, (ids, blocks[0], *got), [((4, 32, HALF), BF)] * 2, spaces={0: SMEM})
    mine = (mine.astype(F32) + shift(other, "zh", 1).astype(F32)).astype(BF)
    piece = jnp.stack([mine, shift(mine, "zh", 1)])
    piece = jnp.stack(collect(piece, 1))
    pieces = collect(piece, 0)
    pieces = pieces + [shift(p, "core", 1) for p in pieces]
    whole = lambda p: pl.BlockSpec(p.shape, lambda i, n=p.ndim: (0,) * n)
    total_qkv, total_out = pl.pallas_call(
        final_attn,
        grid=(4,),
        out_shape=[jax.ShapeDtypeStruct((D, 3 * D), F32), jax.ShapeDtypeStruct((D, D), F32)],
        in_specs=[pl.BlockSpec(memory_space=SMEM)] + [whole(p) for p in pieces],
        out_specs=[pl.BlockSpec((256, 3 * D), lambda i: (i, 0)), pl.BlockSpec((256, D), lambda i: (i, 0))],
        compiler_params=pltpu.CompilerParams(vmem_limit_bytes=VMEM_BYTES),
    )(ids, *pieces)
    total_gain = small_sum(jnp.where(first, encoder_gain, latent_gain))
    return (
        patch_out.reshape(1, micro, 1, seq, D),
        byte_grad.reshape(micro, 1, half_bytes, D),
        total_qkv[None],
        total_out[None],
        total_gain[None],
        ff_grad[None],
    )


def solution(mesh):
    fine = Mesh(mesh.devices.reshape(2, 4, 4, 2, 2), ("s",) + BATCH)
    in_specs = (
        P("s", None, BATCH, None, None),
        P(None, BATCH, "s", None),
        P(None, BATCH, None),
        P(None, BATCH, None),
        P("s", None, None),
        P("s", None, None),
        P("s", None, None),
        P(),
    )
    out_specs = (
        P("s", None, BATCH, None, None),
        P(None, BATCH, "s", None),
        P("s", None, None),
        P("s", None, None),
        P("s", None, None),
        P("s", BATCH, None, None),
    )
    return jax.shard_map(shards, mesh=fine, in_specs=in_specs, out_specs=out_specs, check_vma=False)
```

time: 574 us -> 350 us (0.61)
  local copies, waits for them, and re-layouts: 153 us -> 4.73 us
  Pallas kernels: 0 us -> 76.8 us
  other arithmetic: 68 us -> 9.77 us
  matrix products: 54.9 us -> 0 us
  waiting for transfers between devices: 179 us -> 142 us
    pallas_call x0 -> x14, Pallas kernels: none -> 76.8 us  [the longest x8 67.1 us: call(): pl.pallas_call(kernel, out_shape=[jax.ShapeDtypeStruct(s, t) for s, t in...]
    ppermute x71 -> x20, starting transfers between devices: 95.9 us -> 38.9 us  [shift(): lax.ppermute(value, axis, [(i, (i + by) % size) for i in range(size)])]
    dot_general x18 -> x0, matrix products: 54.9 us -> none  [the longest x4 15.2 us: dot_t(): return jnp.einsum('sc,dc->sd', left, right, preferred_element_type=F32)]
    ppermute x4, waiting for transfers between devices: 91.3 us -> 50.6 us  [along(): return lax.ppermute(value, 's', [(0, 1)] if by > 0 else [(1, 0)])]
    reshape x14 -> x1, local copies, waits for them, and re-layouts: 40.6 us -> 0.05 us  [shards(): (ff_own.astype(F32) + ff_far.astype(F32)).astype(BF)]
    slice x41 -> x0, local copies, waits for them, and re-layouts: 38.7 us -> none  [the longest x2 24 us: shards(): total_qkv = jnp.swapaxes(gathered[:3], 0, 1).reshape(width, 3 * width)]
    ppermute x4, starting transfers between devices: 5.23 us -> 43.3 us  [along(): return lax.ppermute(value, 's', [(0, 1)] if by > 0 else [(1, 0)])]
    ppermute x0 -> x18, waiting for transfers between devices: none -> 34.2 us  [plane_shift(): return lax.ppermute(value, ('s', 'y', 'x', 'core'), pairs)]
  transfers between devices with their start and end apart: 75 -> 42, of which waited for: 31 -> 21; matrix products, arithmetic and copies ran while one was open for 27% -> 4% of each run, Pallas kernels for 0% -> 11%
where the time goes in v2:
time: 350 us; the launch traced here: 344 us
  waiting for transfers between devices  142 us (41%)
  starting transfers between devices  100 us (29%)
  Pallas kernels  76.8 us (22%)
  other arithmetic  9.77 us (3%)
  loops' own time  8.83 us (3%)
  local copies, waits for them, and re-layouts  4.73 us (1%)
    pallas_call x8, Pallas kernels, call(): pl.pallas_call(kernel, out_shape=[jax.ShapeDtypeStruct(s, t) for s, t in...  67.1 us
    ppermute x20, waiting for transfers between devices, shift(): lax.ppermute(value, axis, [(i, (i + by) % size) for i in range(size)])  57.6 us
    ppermute x4, waiting for transfers between devices, along(): return lax.ppermute(value, 's', [(0, 1)] if by > 0 else [(1, 0)])  50.6 us
    ppermute x4, starting transfers between devices, along(): return lax.ppermute(value, 's', [(0, 1)] if by > 0 else [(1, 0)])  43.3 us
    ppermute x20, starting transfers between devices, shift(): lax.ppermute(value, axis, [(i, (i + by) % size) for i in range(size)])  38.9 us
    ppermute x18, waiting for transfers between devices, plane_shift(): return lax.ppermute(value, ('s', 'y', 'x', 'core'), pairs)  34.2 us
    ppermute x18, starting transfers between devices, plane_shift(): return lax.ppermute(value, ('s', 'y', 'x', 'core'), pairs)  18.1 us
    pallas_call x1, Pallas kernels, shards(): pl.pallas_call(final_attn, grid=(4,), out_shape=[jax.ShapeDtypeStruct((D,...  9.65 us
  transfers between devices with their start and end apart: 42, of which 21 were waited for; matrix products, arithmetic and copies ran while one was open for 4% of the time, Pallas kernels for 11%

profile of v2, /device:TPU:7, one launch (start us, length us, event | category | flops | bytes accessed | tf_op | source)
XLA Modules:
  0.0 344.0 jit_solution(9437868452452776112)
XLA Ops:
  0.6 1.3 collective-permute-start
  2.0 1.1 reduce_window_sum.11
  3.8 7.1 %conditional.11 = ((bf16[128,1024]{1,0:T(8,128)(2,1)}, bf16[128,1024]{1,0:T(8,128)(2,1)S(1)}, bf16[512,1024]{1,0:T(8,128)(2,1)}, bf16[512,1024]{1,0:T(8,128)(2,1)S(1)}, bf16[512,1024]{1,0:T(8,128)(2,1)})) conditional(s32[]{:T(128)} %convert_element_type.51, () %tuple.89, (bf16[128,1024]{1,0:T(8,128)(2,1)}, bf16[512,1024]{1,0:T(8,128)(2,1)}, ...), branch_computations={%region_1.2_spmd, %region_2.3_spmd} | conditional | bytes 8 | solution.py:443
  3.8 7.1 %branch_1_fun.12 = (bf16[128,1024]{1,0:T(8,128)(2,1)}, bf16[128,1024]{1,0:T(8,128)(2,1)S(1)}, bf16[512,1024]{1,0:T(8,128)(2,1)}, bf16[512,1024]{1,0:T(8,128)(2,1)S(1)}, bf16[512,1024]{1,0:T(8,128)(2,1)}) custom-call(bf16[128,1024]{1,0:T(8,128)(2,1)} %get-tuple-element.197.patch, bf16[512,1024]{1,0:T(8,128)(2,1)} %get-tuple-element.198.low, ...), custom_call_target="tpu_custom_call" | custom-call | tf_op jit(solution)/shard_map/cond/branch_1_fun/pallas_call | solution.py:420
  10.9 16.0 %collective-permute-done = bf16[512,1024]{1,0:T(8,128)(2,1)} collective-permute-done((bf16[512,1024]{1,0:T(8,128)(2,1)}, bf16[512,1024]{1,0:T(8,128)(2,1)}, u32[]{:S(2)}, u32[]{:S(2)}) %collective-permute-start) | collective-permute-done | bytes 1048608 | tf_op jit(solution)/shard_map/ppermute | solution.py:454
  26.9 10.9 %conditional.12 = ((bf16[128,1024]{1,0:T(8,128)(2,1)}, bf16[128,1024]{1,0:T(8,128)(2,1)}, bf16[16,256,256]{2,1,0:T(8,128)(2,1)}, bf16[512,1024]{1,0:T(8,128)(2,1...) conditional(s32[]{:T(128)} %convert_element_type.51, () %tuple.88, (s32[2,2,64]{2,1,0:T(2,128)S(1)}, ...), branch_computations={%region_3.4_spmd, %region_4.5_spmd} | conditional | bytes 13320 | solution.py:443
  27.6 10.2 %branch_1_fun.13 = (bf16[128,1024]{1,0:T(8,128)(2,1)}, bf16[128,1024]{1,0:T(8,128)(2,1)}, bf16[16,256,256]{2,1,0:T(8,128)(2,1)}, bf16[512,1024]{1,0:T(8,128)(2,1...) custom-call(bf16[128,1024]{1,0:T(8,128)(2,1)} %get-tuple-element.201.patch, ...), custom_call_target="tpu_custom_call" | custom-call | tf_op jit(solution)/shard_map/cond/branch_1_fun/pallas_call | solution.py:420
  37.8 2.0 collective-permute-start.1
  40.0 3.8 %collective-permute-done.1 = bf16[128,1024]{1,0:T(8,128)(2,1)} collective-permute-done((bf16[128,1024]{1,0:T(8,128)(2,1)}, bf16[128,1024]{1,0:T(8,128)(2,1)}, u32[]{:S(2)}, u32[]{:S(2)}) %collective-permute-start.1) | collective-permute-done | bytes 262176 | tf_op jit(solution)/shard_map/ppermute | solution.py:454
  43.7 8.2 %conditional.13 = ((f32[128,1024]{1,0:T(8,128)}, bf16[128,1024]{1,0:T(8,128)(2,1)}, f32[2,1024]{1,0:T(2,128)S(1)}, bf16[128,1024]{1,0:T(8,128)(2,1)}, bf16[128,1...) conditional(s32[]{:T(128)} %convert_element_type.52, () %tuple.87, ...), branch_computations={%region_5.6_spmd, %region_6.7_spmd} | conditional | bytes 425992 | solution.py:443
  51.9 1.3 collective-permute-start.2
  53.2 30.9 %collective-permute-done.2 = bf16[128,1024]{1,0:T(8,128)(2,1)} collective-permute-done((bf16[128,1024]{1,0:T(8,128)(2,1)}, bf16[128,1024]{1,0:T(8,128)(2,1)}, u32[]{:S(2)}, u32[]{:S(2)}) %collective-permute-start.2) | collective-permute-done | bytes 262176 | tf_op jit(solution)/shard_map/ppermute | solution.py:454
  84.1 17.9 %conditional.14 = ((bf16[2304,512]{1,0:T(8,128)(2,1)}, bf16[2304,512]{1,0:T(8,128)(2,1)})) conditional(s32[]{:T(128)} %convert_element_type.51, () %tuple.93, (s32[4]{0:T(128)S(1)}, bf16[128,1024]{1,0:T(8,128)(2,1)}, bf16[1024,1024]{1,0:T(8,128)(2,1)S(1)}, bf16[128,1024]{1,0:T(8,128)(2,1)S(1)}, bf16[512,1024]{1,0:T(8,128)(2,1)S(1)}, ...), branch_computations={%region_7.8_spmd, %region_8.9_spmd} | conditional | bytes 8 | solution.py:443
  84.1 17.9 %branch_1_fun.15 = (bf16[2304,512]{1,0:T(8,128)(2,1)}, bf16[2304,512]{1,0:T(8,128)(2,1)}) custom-call(s32[4]{0:T(128)S(1)} %get-tuple-element.218.ids, bf16[128,1024]{1,0:T(8,128)(2,1)} %get-tuple-element.219.dhb, bf16[1024,1024]{1,0:T(8,128)(2,1)S(1)} %get-tuple-element.220.w_out, bf16[128,1024]{1,0:T(8,128)(2,1)S(1)} %get-tuple-element.221.q, ...), custom_call_target="tpu_custom_call" | custom-call | tf_op jit(solution)/shard_map/cond/branch_1_fun/pallas_call | solution.py:420
  101.9 2.8 collective-permute-start.7
  104.8 3.9 %conditional.16 = ((bf16[2048,128]{1,0:T(8,128)(2,1)S(1)}, bf16[1024,1024]{1,0:T(8,128)(2,1)})) conditional(s32[]{:T(128)} %convert_element_type.51, (bf16[128,1024]{1,0:T(8,128)(2,1)}, bf16[128,1024]{1,0:T(8,128)(2,1)}) %tuple.96, (bf16[128,1024]{1,0:T(8,128)(2,1)}, bf16[128,1024]{1,0:T(8,128)(2,1)}, bf16[512,1024]{1,0:T(8,128)(2,1)}, ...), branch_computations={%region_11.12_spmd, %region_12.13_spmd} | conditional | bytes 24 | solution.py:549
  104.8 3.9 %branch_1_fun.17 = (bf16[2048,128]{1,0:T(8,128)(2,1)S(1)}, bf16[1024,1024]{1,0:T(8,128)(2,1)}) custom-call(bf16[128,1024]{1,0:T(8,128)(2,1)} %get-tuple-element.238.pn, bf16[128,1024]{1,0:T(8,128)(2,1)} %get-tuple-element.239.o1, bf16[512,1024]{1,0:T(8,128)(2,1)} %get-tuple-element.240.bn_lo, bf16[512,1024]{1,0:T(8,128)(2,1)} %get-tuple-element.241.bn_up), custom_call_target="tpu_custom_call" | custom-call | tf_op jit(solution)/shard_map/cond/branch_1_fun/pallas_call | solution.py:420
  109.7 7.7 %collective-permute-done.4 = bf16[2048,128]{1,0:T(8,128)(2,1)S(1)} collective-permute-done((bf16[2048,128]{1,0:T(8,128)(2,1)S(1)}, bf16[2048,128]{1,0:T(8,128)(2,1)S(1)}, u32[]{:S(2)}, u32[]{:S(2)}) %collective-permute-start.4) | collective-permute-done | bytes 524320 | tf_op jit(solution)/shard_map/ppermute | solution.py:450
  117.6 10.4 %conditional.17 = ((bf16[4,256,512]{2,1,0:T(8,128)(2,1)}, bf16[4,256,512]{2,1,0:T(8,128)(2,1)}, bf16[4,256,512]{2,1,0:T(8,128)(2,1)}, bf16[4,256,512]{2,1,0:T(8,128)(2,1)})) conditional(s32[]{:T(128)} %convert_element_type.51, (s32[4]{0:T(128)S(1)}, bf16[2048,128]{1,0:T(8,128)(2,1)S(1)}, bf16[2048,128]{1,0:T(8,128)(2,1)S(1)}, ...), branch_computations={%region_13.14_spmd, %region_14.15_spmd} | conditional | bytes 8 | solution.py:592
  117.8 10.2 %branch_1_fun.18 = (bf16[4,256,512]{2,1,0:T(8,128)(2,1)}, bf16[4,256,512]{2,1,0:T(8,128)(2,1)}, bf16[4,256,512]{2,1,0:T(8,128)(2,1)}, bf16[4,256,512]{2,1,0:T(8,128)(2,1)}) custom-call(s32[4]{0:T(128)S(1)} %get-tuple-element.247.ids, bf16[2048,128]{1,0:T(8,128)(2,1)S(1)} %get-tuple-element.248.left, bf16[2048,128]{1,0:T(8,128)(2,1)S(1)} %get-tuple-element.249.left_far, ...), custom_call_target="tpu_custom_call" | custom-call | tf_op jit(solution)/shard_map/cond/branch_1_fun/pallas_call | solution.py:420
  129.0 1.8 collective-permute-start.33
  130.7 1.2 collective-permute-done.33
  132.7 2.0 collective-permute-start.35
  134.7 2.0 collective-permute-start.36
  136.7 1.1 collective-permute-start.9
  137.9 4.4 %collective-permute-done.8.a = bf16[4,256,512]{2,1,0:T(8,128)(2,1)} collective-permute-done((bf16[4,256,512]{2,1,0:T(8,128)(2,1)}, bf16[4,256,512]{2,1,0:T(8,128)(2,1)}, u32[]{:S(2)}, u32[]{:S(2)}) %collective-permute-start.8) | collective-permute-done | bytes 1048608 | tf_op jit(solution)/shard_map/ppermute | solution.py:465
  142.8 9.6 %collective-permute-done.9.b = bf16[4,256,512]{2,1,0:T(8,128)(2,1)S(1)} collective-permute-done((bf16[4,256,512]{2,1,0:T(8,128)(2,1)}, bf16[4,256,512]{2,1,0:T(8,128)(2,1)S(1)}, u32[]{:S(2)}, u32[]{:S(2)}) %collective-permute-start.9) | collective-permute-done | bytes 1048608 | tf_op jit(solution)/shard_map/ppermute | solution.py:465
  152.4 11.0 %collective-permute-done.10.c = bf16[4,256,512]{2,1,0:T(8,128)(2,1)} collective-permute-done((bf16[4,256,512]{2,1,0:T(8,128)(2,1)}, bf16[4,256,512]{2,1,0:T(8,128)(2,1)}, u32[]{:S(2)}, u32[]{:S(2)}) %collective-permute-start.10) | collective-permute-done | bytes 1048608 | tf_op jit(solution)/shard_map/ppermute | solution.py:465
  163.4 3.4 shard_map.127
  166.9 1.3 collective-permute-start.11
  168.1 1.8 collective-permute-start.12
  169.9 3.9 %collective-permute-done.11.a = bf16[4,64,512]{2,1,0:T(8,128)(2,1)S(1)} collective-permute-done((bf16[4,64,512]{2,1,0:T(8,128)(2,1)}, bf16[4,64,512]{2,1,0:T(8,128)(2,1)S(1)}, u32[]{:S(2)}, u32[]{:S(2)}) %collective-permute-start.11) | collective-permute-done | bytes 262176 | tf_op jit(solution)/shard_map/ppermute | solution.py:465
  174.2 2.5 collective-permute-done.12.b
  176.7 2.8 collective-permute-done.13.c
  180.2 2.0 shard_map.128
  182.2 3.6 %collective-permute-start.14 = (bf16[4,32,512]{2,1,0:T(8,128)(2,1)}, bf16[4,32,512]{2,1,0:T(8,128)(2,1)S(1)}, u32[]{:S(2)}, u32[]{:S(2)}) collective-permute-start(bf16[4,32,512]{2,1,0:T(8,128)(2,1)} %get-tuple-element.356), channel_id=1, source_target_pairs={{0,2},{2,0},{1,3},{3,1},{4,6},{6,4},{5,7},{7,5},{8,10},{10,8},{9,1... | collective-permute-start | bytes 393224 | tf_op jit(solution)/shard_map/ppermute | solution.py:450
  185.8 2.6 collective-permute-done.14
  188.4 1.6 add_convert_fusion
  190.0 3.0 collective-permute-start.15
  194.1 1.5 collective-permute-done.15
  196.6 1.5 collective-permute-start.17
  198.1 1.5 collective-permute-start.16
  200.1 12.5 %conditional.15 = ((f32[128,1024]{1,0:T(8,128)}, bf16[512,1024]{1,0:T(8,128)(2,1)}, bf16[512,1024]{1,0:T(8,128)(2,1)}, f32[2,1024]{1,0:T(2,128)S(1)})) conditional(s32[]{:T(128)} %convert_element_type.51, () %tuple.86, (s32[4]{0:T(128)S(1)}, bf16[128,1024]{1,0:T(8,128)(2,1)}, bf16[128,1024]{1,0:T(8,128)(2,1)S(1)}, bf16[512,1024]{1,0:T(8,128)(2,1)S(1)}, ...), branch_computations={%region_9.10_spmd, %region_10.11_spmd} | conditional | bytes 8 | solution.py:443
  200.2 12.5 %branch_1_fun.16 = (f32[128,1024]{1,0:T(8,128)}, bf16[512,1024]{1,0:T(8,128)(2,1)}, bf16[512,1024]{1,0:T(8,128)(2,1)}, f32[2,1024]{1,0:T(2,128)S(1)}) custom-call(s32[4]{0:T(128)S(1)} %get-tuple-element.227.ids, bf16[128,1024]{1,0:T(8,128)(2,1)} %get-tuple-element.228.dhb, bf16[128,1024]{1,0:T(8,128)(2,1)S(1)} %get-tuple-element.229.patch, ...), custom_call_target="tpu_custom_call" | custom-call | tf_op jit(solution)/shard_map/cond/branch_1_fun/pallas_call | solution.py:420
  212.7 5.2 %collective-permute-start.26 = (f32[2,1024]{1,0:T(2,128)S(1)}, f32[2,1024]{1,0:T(2,128)S(1)}, u32[]{:S(2)}, u32[]{:S(2)}) collective-permute-start(f32[2,1024]{1,0:T(2,128)S(1)} %broadcast_select_fusion.2), channel_id=1, source_target_pairs={{0,1},{1,0},{2,3},{3,2},{4,5},{5,4},{6,7},{7,6},{8,9},{9,8},{10,11... | collective-permute-start | bytes 24584 | tf_op jit(solution)/shard_map/ppermute | solution.py:450
  218.4 1.1 collective-permute-start.20
  219.8 3.3 collective-permute-start.27
  223.2 1.0 collective-permute-done.27
  224.2 2.4 collective-permute-start.28
  226.6 17.0 %collective-permute-done.28 = f32[2,1024]{1,0:T(2,128)S(1)} collective-permute-done((f32[2,1024]{1,0:T(2,128)S(1)}, f32[2,1024]{1,0:T(2,128)S(1)}, u32[]{:S(2)}, u32[]{:S(2)}) %collective-permute-start.28) | collective-permute-done | bytes 8224 | tf_op jit(solution)/shard_map/ppermute | solution.py:450
  244.5 3.5 %collective-permute-done.29 = f32[2,1024]{1,0:T(2,128)S(1)} collective-permute-done((f32[2,1024]{1,0:T(2,128)S(1)}, f32[2,1024]{1,0:T(2,128)S(1)}, u32[]{:S(2)}, u32[]{:S(2)}) %collective-permute-start.29) | collective-permute-done | bytes 8224 | tf_op jit(solution)/shard_map/ppermute | solution.py:450
  248.1 6.1 %collective-permute-start.30 = (f32[2,1024]{1,0:T(2,128)S(1)}, f32[2,1024]{1,0:T(2,128)S(1)}, u32[]{:S(2)}, u32[]{:S(2)}) collective-permute-start(f32[2,1024]{1,0:T(2,128)S(1)} %add.47), channel_id=1, source_target_pairs={{0,16},{16,32},{32,48},{48,0},{1,17},{17,33},{33,49},{49,1},{2,18}... | collective-permute-start | bytes 24584 | tf_op jit(solution)/shard_map/ppermute | solution.py:450
  254.1 1.2 collective-permute-done.30
  256.0 1.5 collective-permute-start.39
  257.5 38.8 %collective-permute-start.3 = (bf16[512,1024]{1,0:T(8,128)(2,1)}, bf16[512,1024]{1,0:T(8,128)(2,1)}, u32[]{:S(2)}, u32[]{:S(2)}) collective-permute-start(bf16[512,1024]{1,0:T(8,128)(2,1)} %get-tuple-element.336), channel_id=1, source_target_pairs={{0,64},{1,65},{2,66},{3,67},{4,68},{5,69},{6,70},{7,71},{8,72},{9,... | collective-permute-start | bytes 3145736 | tf_op jit(solution)/shard_map/ppermute | solution.py:454
  296.3 3.1 collective-permute-start.31
  299.4 1.0 collective-permute-done.31
  301.0 1.9 broadcast_select_fusion.1
  302.9 19.1 %collective-permute-done.40 = bf16[3,88,512]{2,1,0:T(8,128)(2,1)S(1)} collective-permute-done((bf16[3,88,512]{2,1,0:T(8,128)(2,1)S(1)}, bf16[3,88,512]{2,1,0:T(8,128)(2,1)S(1)}, u32[]{:S(2)}, u32[]{:S(2)}) %collective-permute-start.40) | collective-permute-done | bytes 270368 | tf_op jit(solution)/shard_map/ppermute | solution.py:450
  322.0 4.0 %collective-permute-start.22 = (bf16[4,2,4,32,512]{4,3,2,1,0:T(8,128)(2,1)S(1)}, bf16[4,2,4,32,512]{4,3,2,1,0:T(8,128)(2,1)}, u32[]{:S(2)}, u32[]{:S(2)}) collective-permute-start(bf16[4,2,4,32,512]{4,3,2,1,0:T(8,128)(2,1)S(1)} %pad_maximum_fusion.refs_0_), channel_id=1, source_target_pairs={{0,1},{1,0},{2,3},{3,2},{4,5},{5,4},{6,7},{7,6},{8,9},{9,8},{10,11... | collective-permute-start | bytes 3145736 | tf_op jit(solution)/shard_map/ppermute | solution.py:450
  328.0 2.3 broadcast_select_fusion
  330.3 1.5 collective-permute-done.41
  332.8 1.4 copy.18
  334.1 9.6 %shard_map.129 = (f32[1024,3072]{1,0:T(8,128)}, f32[1024,1024]{1,0:T(8,128)}) custom-call(s32[4]{0:T(128)S(1)} %pad_add_fusion.1.ids, bf16[4,2,4,32,512]{4,3,2,1,0:T(8,128)(2,1)} %copy-done.2, bf16[4,2,4,32,512]{4,3,2,1,0:T(8,128)(2,1)} %collective-permute-done.19.refs_1_, bf16[4,2,4,32,512]{4,3,2,1,0:T(8,128)(2,1)} %collective-permute-done.20.refs_2_, ...), custom_call_target="tpu_custom_call" | custom-call | tf_op jit(solution)/shard_map/pallas_call | solution.py:625
  (99 shorter events, 14.7 us)
Async XLA Ops:
  0.6 26.2 %collective-permute-start = (bf16[512,1024]{1,0:T(8,128)(2,1)}, bf16[512,1024]{1,0:T(8,128)(2,1)}, u32[]{:S(2)}, u32[]{:S(2)}) collective-permute-start(bf16[512,1024]{1,0:T(8,128)(2,1)} %bitcast.66), channel_id=1, source_target_pairs={{64,0},{65,1},{66,2},{67,3},{68,4},{69,5},{70,6},{71,7},{72,8},{73... | collective-permute-start | bytes 3145736 | tf_op jit(solution)/shard_map/ppermute | solution.py:454
  3.8 7.1 %copy-start.11 = (s32[2,1,64]{2,1,0:T(1,128)S(1)}, s32[2,1,64]{2,1,0:T(1,128)}, u32[]{:S(2)}) copy-start(s32[2,1,64]{2,1,0:T(1,128)} %param.33) | copy-start | bytes 1540
  3.8 23.1 %copy-start = (bf16[1,1024,1024]{2,1,0:T(8,128)(2,1)S(1)}, bf16[1,1024,1024]{2,1,0:T(8,128)(2,1)}, u32[]{:S(2)}) copy-start(bf16[1,1024,1024]{2,1,0:T(8,128)(2,1)} %param.35) | copy-start | bytes 6291460
  37.8 5.9 %collective-permute-start.1 = (bf16[128,1024]{1,0:T(8,128)(2,1)}, bf16[128,1024]{1,0:T(8,128)(2,1)}, u32[]{:S(2)}, u32[]{:S(2)}) collective-permute-start(bf16[128,1024]{1,0:T(8,128)(2,1)} %get-tuple-element.326), channel_id=1, source_target_pairs={{0,64},{1,65},{2,66},{3,67},{4,68},{5,69},{6,70},{7,71},{8,72},{9,... | collective-permute-start | bytes 786440 | tf_op jit(solution)/shard_map/ppermute | solution.py:454
  51.9 32.2 %collective-permute-start.2 = (bf16[128,1024]{1,0:T(8,128)(2,1)}, bf16[128,1024]{1,0:T(8,128)(2,1)}, u32[]{:S(2)}, u32[]{:S(2)}) collective-permute-start(bf16[128,1024]{1,0:T(8,128)(2,1)} %get-tuple-element.327), channel_id=1, source_target_pairs={{64,0},{65,1},{66,2},{67,3},{68,4},{69,5},{70,6},{71,7},{72,8},{73... | collective-permute-start | bytes 786440 | tf_op jit(solution)/shard_map/ppermute | solution.py:454
  101.9 15.7 %collective-permute-start.7 = (bf16[2304,512]{1,0:T(8,128)(2,1)}, bf16[2304,512]{1,0:T(8,128)(2,1)}, u32[]{:S(2)}, u32[]{:S(2)}) collective-permute-start(bf16[2304,512]{1,0:T(8,128)(2,1)} %get-tuple-element.332), channel_id=1, source_target_pairs={{0,1},{1,0},{2,3},{3,2},{4,5},{5,4},{6,7},{7,6},{8,9},{9,8},{10,11... | collective-permute-start | bytes 7077896 | tf_op jit(solution)/shard_map/ppermute | solution.py:450
  108.6 9.0 %collective-permute-start.6 = (bf16[1024,1024]{1,0:T(8,128)(2,1)}, bf16[1024,1024]{1,0:T(8,128)(2,1)}, u32[]{:S(2)}, u32[]{:S(2)}) collective-permute-start(bf16[1024,1024]{1,0:T(8,128)(2,1)} %get-tuple-element.346), channel_id=1, source_target_pairs={{0,1},{1,0},{2,3},{3,2},{4,5},{5,4},{6,7},{7,6},{8,9},{9,8},{10,11... | collective-permute-start | bytes 6291464 | tf_op jit(solution)/shard_map/ppermute | solution.py:450
  108.6 23.3 %collective-permute-start.32 = (bf16[8448,128]{1,0:T(8,128)(2,1)S(1)}, bf16[8448,128]{1,0:T(8,128)(2,1)}, u32[]{:S(2)}, u32[]{:S(2)}) collective-permute-start(bf16[8448,128]{1,0:T(8,128)(2,1)S(1)} %get-tuple-element.470), channel_id=1, source_target_pairs={{0,1},{1,0},{2,3},{3,2},{4,5},{5,4},{6,7},{7,6},{8,9},{9,8},{10,11... | collective-permute-start | bytes 6488072 | tf_op jit(solution)/shard_map/ppermute | solution.py:450
  109.1 8.2 %collective-permute-start.4 = (bf16[2048,128]{1,0:T(8,128)(2,1)S(1)}, bf16[2048,128]{1,0:T(8,128)(2,1)S(1)}, u32[]{:S(2)}, u32[]{:S(2)}) collective-permute-start(bf16[2048,128]{1,0:T(8,128)(2,1)S(1)} %get-tuple-element.343), channel_id=1, source_target_pairs={{0,1},{1,0},{2,3},{3,2},{4,5},{5,4},{6,7},{7,6},{8,9},{9,8},{10,11... | collective-permute-start | bytes 1572872 | tf_op jit(solution)/shard_map/ppermute | solution.py:450
  109.1 8.4 %collective-permute-start.5 = (bf16[512,512]{1,0:T(8,128)(2,1)}, bf16[512,512]{1,0:T(8,128)(2,1)S(1)}, u32[]{:S(2)}, u32[]{:S(2)}) collective-permute-start(bf16[512,512]{1,0:T(8,128)(2,1)} %get-tuple-element.345), channel_id=1, source_target_pairs={{0,1},{1,0},{2,3},{3,2},{4,5},{5,4},{6,7},{7,6},{8,9},{9,8},{10,11... | collective-permute-start | bytes 1572872 | tf_op jit(solution)/shard_map/ppermute | solution.py:450
  128.0 14.3 %collective-permute-start.8 = (bf16[4,256,512]{2,1,0:T(8,128)(2,1)}, bf16[4,256,512]{2,1,0:T(8,128)(2,1)}, u32[]{:S(2)}, u32[]{:S(2)}) collective-permute-start(bf16[4,256,512]{2,1,0:T(8,128)(2,1)} %get-tuple-element.348), channel_id=1, source_target_pairs={{0,16},{1,5},{4,20},{5,9},{8,24},{9,13},{12,28},{13,1},{16,32},{17... | collective-permute-start | bytes 3145736 | tf_op jit(solution)/shard_map/ppermute | solution.py:465
  129.0 3.0 collective-permute-start.33
  131.9 61.0 %collective-permute-start.34 = (bf16[4,528,512]{2,1,0:T(8,128)(2,1)}, bf16[4,528,512]{2,1,0:T(8,128)(2,1)S(1)}, u32[]{:S(2)}, u32[]{:S(2)}) collective-permute-start(bf16[4,528,512]{2,1,0:T(8,128)(2,1)} %get-tuple-element.364), channel_id=1, source_target_pairs={{64,80},{65,69},{68,84},{69,73},{72,88},{73,77},{76,92},{77,65},{8... | collective-permute-start | bytes 6488072 | tf_op jit(solution)/shard_map/ppermute | solution.py:465
  132.7 60.2 %collective-permute-start.35 = (bf16[4,528,512]{2,1,0:T(8,128)(2,1)}, bf16[4,528,512]{2,1,0:T(8,128)(2,1)}, u32[]{:S(2)}, u32[]{:S(2)}) collective-permute-start(bf16[4,528,512]{2,1,0:T(8,128)(2,1)} %get-tuple-element.365), channel_id=1, source_target_pairs={{64,96},{65,73},{68,100},{69,77},{72,104},{73,65},{76,108},{77,69}... | collective-permute-start | bytes 6488072 | tf_op jit(solution)/shard_map/ppermute | solution.py:465
  134.7 58.2 %collective-permute-start.36 = (bf16[4,528,512]{2,1,0:T(8,128)(2,1)}, bf16[4,528,512]{2,1,0:T(8,128)(2,1)}, u32[]{:S(2)}, u32[]{:S(2)}) collective-permute-start(bf16[4,528,512]{2,1,0:T(8,128)(2,1)} %get-tuple-element.366), channel_id=1, source_target_pairs={{64,112},{65,77},{68,116},{69,65},{72,120},{73,69},{76,124},{77,73... | collective-permute-start | bytes 6488072 | tf_op jit(solution)/shard_map/ppermute | solution.py:465
  136.7 15.7 %collective-permute-start.9 = (bf16[4,256,512]{2,1,0:T(8,128)(2,1)}, bf16[4,256,512]{2,1,0:T(8,128)(2,1)S(1)}, u32[]{:S(2)}, u32[]{:S(2)}) collective-permute-start(bf16[4,256,512]{2,1,0:T(8,128)(2,1)} %get-tuple-element.349), channel_id=1, source_target_pairs={{0,32},{1,9},{4,36},{5,13},{8,40},{9,1},{12,44},{13,5},{16,48},{17... | collective-permute-start | bytes 3145736 | tf_op jit(solution)/shard_map/ppermute | solution.py:465
  142.2 21.2 %collective-permute-start.10 = (bf16[4,256,512]{2,1,0:T(8,128)(2,1)}, bf16[4,256,512]{2,1,0:T(8,128)(2,1)}, u32[]{:S(2)}, u32[]{:S(2)}) collective-permute-start(bf16[4,256,512]{2,1,0:T(8,128)(2,1)} %get-tuple-element.350), channel_id=1, source_target_pairs={{0,48},{1,13},{4,52},{5,1},{8,56},{9,5},{12,60},{13,9},{16,0},{17,... | collective-permute-start | bytes 3145736 | tf_op jit(solution)/shard_map/ppermute | solution.py:465
  152.4 11.0 %copy-start.5 = (bf16[4,256,512]{2,1,0:T(8,128)(2,1)}, bf16[4,256,512]{2,1,0:T(8,128)(2,1)S(1)}, u32[]{:S(2)}) copy-start(bf16[4,256,512]{2,1,0:T(8,128)(2,1)S(1)} %collective-permute-done.9.b) | copy-start | bytes 3145732
  166.9 6.9 %collective-permute-start.11 = (bf16[4,64,512]{2,1,0:T(8,128)(2,1)}, bf16[4,64,512]{2,1,0:T(8,128)(2,1)S(1)}, u32[]{:S(2)}, u32[]{:S(2)}) collective-permute-start(bf16[4,64,512]{2,1,0:T(8,128)(2,1)} %get-tuple-element.352), channel_id=1, source_target_pairs={{0,4},{1,17},{4,8},{5,21},{8,12},{9,25},{12,0},{13,29},{16,20},{17... | collective-permute-start | bytes 786440 | tf_op jit(solution)/shard_map/ppermute | solution.py:465
  168.1 8.6 %collective-permute-start.12 = (bf16[4,64,512]{2,1,0:T(8,128)(2,1)}, bf16[4,64,512]{2,1,0:T(8,128)(2,1)S(1)}, u32[]{:S(2)}, u32[]{:S(2)}) collective-permute-start(bf16[4,64,512]{2,1,0:T(8,128)(2,1)} %get-tuple-element.353), channel_id=1, source_target_pairs={{0,8},{1,33},{4,12},{5,37},{8,0},{9,41},{12,4},{13,45},{16,24},{17... | collective-permute-start | bytes 786440 | tf_op jit(solution)/shard_map/ppermute | solution.py:465
  173.8 5.7 %copy-start.7 = (bf16[4,64,512]{2,1,0:T(8,128)(2,1)}, bf16[4,64,512]{2,1,0:T(8,128)(2,1)S(1)}, u32[]{:S(2)}) copy-start(bf16[4,64,512]{2,1,0:T(8,128)(2,1)S(1)} %collective-permute-done.11.a) | copy-start | bytes 786436
  173.8 5.7 %collective-permute-start.13 = (bf16[4,64,512]{2,1,0:T(8,128)(2,1)}, bf16[4,64,512]{2,1,0:T(8,128)(2,1)S(1)}, u32[]{:S(2)}, u32[]{:S(2)}) collective-permute-start(bf16[4,64,512]{2,1,0:T(8,128)(2,1)} %get-tuple-element.354), channel_id=1, source_target_pairs={{0,12},{1,49},{4,0},{5,53},{8,4},{9,57},{12,8},{13,61},{16,28},{17... | collective-permute-start | bytes 786440 | tf_op jit(solution)/shard_map/ppermute | solution.py:465
  176.7 2.8 copy-start.8
  179.5 0.7 copy-start.9
  182.2 6.2 %collective-permute-start.14 = (bf16[4,32,512]{2,1,0:T(8,128)(2,1)}, bf16[4,32,512]{2,1,0:T(8,128)(2,1)S(1)}, u32[]{:S(2)}, u32[]{:S(2)}) collective-permute-start(bf16[4,32,512]{2,1,0:T(8,128)(2,1)} %get-tuple-element.356), channel_id=1, source_target_pairs={{0,2},{2,0},{1,3},{3,1},{4,6},{6,4},{5,7},{7,5},{8,10},{10,8},{9,1... | collective-permute-start | bytes 393224 | tf_op jit(solution)/shard_map/ppermute | solution.py:450
  190.0 5.6 %collective-permute-start.15 = (bf16[4,32,512]{2,1,0:T(8,128)(2,1)}, bf16[4,32,512]{2,1,0:T(8,128)(2,1)}, u32[]{:S(2)}, u32[]{:S(2)}) collective-permute-start(bf16[4,32,512]{2,1,0:T(8,128)(2,1)} %add_convert_fusion), channel_id=1, source_target_pairs={{0,2},{2,0},{1,3},{3,1},{4,6},{6,4},{5,7},{7,5},{8,10},{10,8},{9,1... | collective-permute-start | bytes 393224 | tf_op jit(solution)/shard_map/ppermute | solution.py:450
  192.9 7.2 %copy-start.1 = (bf16[1,2,1,64,1024]{4,3,2,1,0:T(8,128)(2,1)S(1)}, bf16[1,2,1,64,1024]{4,3,2,1,0:T(8,128)(2,1)}, u32[]{:S(2)}) copy-start(bf16[1,2,1,64,1024]{4,3,2,1,0:T(8,128)(2,1)} %param.30) | copy-start | bytes 786436
  193.0 7.2 %copy-start.3 = (bf16[2,1,256,1024]{3,2,1,0:T(8,128)(2,1)S(1)}, bf16[2,1,256,1024]{3,2,1,0:T(8,128)(2,1)}, u32[]{:S(2)}) copy-start(bf16[2,1,256,1024]{3,2,1,0:T(8,128)(2,1)} %param.31) | copy-start | bytes 3145732
  193.0 7.2 %copy-start.10 = (f32[1,2,1024]{2,1,0:T(2,128)S(1)}, f32[1,2,1024]{2,1,0:T(2,128)}, u32[]{:S(2)}) copy-start(f32[1,2,1024]{2,1,0:T(2,128)} %param.36) | copy-start | bytes 24580
  193.4 62.6 %collective-permute-start.37 = (bf16[528,512]{1,0:T(8,128)(2,1)}, bf16[528,512]{1,0:T(8,128)(2,1)S(1)}, u32[]{:S(2)}, u32[]{:S(2)}) collective-permute-start(bf16[528,512]{1,0:T(8,128)(2,1)} %get-tuple-element.368), channel_id=1, source_target_pairs={{64,68},{65,81},{68,72},{69,85},{72,76},{73,89},{76,64},{77,93},{8... | collective-permute-start | bytes 1622024 | tf_op jit(solution)/shard_map/ppermute | solution.py:465
  196.6 21.3 %collective-permute-start.17 = (bf16[2,4,32,512]{3,2,1,0:T(8,128)(2,1)S(1)}, bf16[2,4,32,512]{3,2,1,0:T(8,128)(2,1)S(1)}, u32[]{:S(2)}, u32[]{:S(2)}) collective-permute-start(bf16[2,4,32,512]{3,2,1,0:T(8,128)(2,1)S(1)} %get-tuple-element.380), channel_id=1, source_target_pairs={{0,8},{1,33},{4,12},{5,37},{8,0},{9,41},{12,4},{13,45},{16,24},{17... | collective-permute-start | bytes 786440 | tf_op jit(solution)/shard_map/ppermute | solution.py:465
  198.1 19.8 %collective-permute-start.16 = (bf16[2,4,32,512]{3,2,1,0:T(8,128)(2,1)S(1)}, bf16[2,4,32,512]{3,2,1,0:T(8,128)(2,1)S(1)}, u32[]{:S(2)}, u32[]{:S(2)}) collective-permute-start(bf16[2,4,32,512]{3,2,1,0:T(8,128)(2,1)S(1)} %get-tuple-element.380), channel_id=1, source_target_pairs={{0,12},{1,49},{4,0},{5,53},{8,4},{9,57},{12,8},{13,61},{16,28},{17... | collective-permute-start | bytes 786440 | tf_op jit(solution)/shard_map/ppermute | solution.py:465
  199.6 18.2 %collective-permute-start.18 = (bf16[2,4,32,512]{3,2,1,0:T(8,128)(2,1)S(1)}, bf16[2,4,32,512]{3,2,1,0:T(8,128)(2,1)S(1)}, u32[]{:S(2)}, u32[]{:S(2)}) collective-permute-start(bf16[2,4,32,512]{3,2,1,0:T(8,128)(2,1)S(1)} %get-tuple-element.380), channel_id=1, source_target_pairs={{0,4},{1,17},{4,8},{5,21},{8,12},{9,25},{12,0},{13,29},{16,20},{17... | collective-permute-start | bytes 786440 | tf_op jit(solution)/shard_map/ppermute | solution.py:465
  212.7 7.2 %collective-permute-start.26 = (f32[2,1024]{1,0:T(2,128)S(1)}, f32[2,1024]{1,0:T(2,128)S(1)}, u32[]{:S(2)}, u32[]{:S(2)}) collective-permute-start(f32[2,1024]{1,0:T(2,128)S(1)} %broadcast_select_fusion.2), channel_id=1, source_target_pairs={{0,1},{1,0},{2,3},{3,2},{4,5},{5,4},{6,7},{7,6},{8,9},{9,8},{10,11... | collective-permute-start | bytes 24584 | tf_op jit(solution)/shard_map/ppermute | solution.py:450
  218.0 104.0 %copy-start.2 = (bf16[4,2,4,32,512]{4,3,2,1,0:T(8,128)(2,1)}, bf16[4,2,4,32,512]{4,3,2,1,0:T(8,128)(2,1)S(1)}, u32[]{:S(2)}) copy-start(bf16[4,2,4,32,512]{4,3,2,1,0:T(8,128)(2,1)S(1)} %pad_maximum_fusion.refs_0_) | copy-start | bytes 3145732
  218.0 108.0 %collective-permute-start.21 = (bf16[4,2,4,32,512]{4,3,2,1,0:T(8,128)(2,1)S(1)}, bf16[4,2,4,32,512]{4,3,2,1,0:T(8,128)(2,1)S(1)}, u32[]{:S(2)}, u32[]{:S(2)}) collective-permute-start(bf16[4,2,4,32,512]{4,3,2,1,0:T(8,128)(2,1)S(1)} %pad_maximum_fusion.refs_0_), channel_id=1, source_target_pairs={{0,16},{1,5},{4,20},{5,9},{8,24},{9,13},{12,28},{13,1},{16,32},{17... | collective-permute-start | bytes 3145736 | tf_op jit(solution)/shard_map/ppermute | solution.py:465
  218.4 107.7 %collective-permute-start.20 = (bf16[4,2,4,32,512]{4,3,2,1,0:T(8,128)(2,1)S(1)}, bf16[4,2,4,32,512]{4,3,2,1,0:T(8,128)(2,1)}, u32[]{:S(2)}, u32[]{:S(2)}) collective-permute-start(bf16[4,2,4,32,512]{4,3,2,1,0:T(8,128)(2,1)S(1)} %pad_maximum_fusion.refs_0_), channel_id=1, source_target_pairs={{0,32},{1,9},{4,36},{5,13},{8,40},{9,1},{12,44},{13,5},{16,48},{17... | collective-permute-start | bytes 3145736 | tf_op jit(solution)/shard_map/ppermute | solution.py:465
  219.5 107.0 %collective-permute-start.19 = (bf16[4,2,4,32,512]{4,3,2,1,0:T(8,128)(2,1)S(1)}, bf16[4,2,4,32,512]{4,3,2,1,0:T(8,128)(2,1)}, u32[]{:S(2)}, u32[]{:S(2)}) collective-permute-start(bf16[4,2,4,32,512]{4,3,2,1,0:T(8,128)(2,1)S(1)} %pad_maximum_fusion.refs_0_), channel_id=1, source_target_pairs={{0,48},{1,13},{4,52},{5,1},{8,56},{9,5},{12,60},{13,9},{16,0},{17,... | collective-permute-start | bytes 3145736 | tf_op jit(solution)/shard_map/ppermute | solution.py:465
  219.8 4.4 %collective-permute-start.27 = (f32[2,1024]{1,0:T(2,128)S(1)}, f32[2,1024]{1,0:T(2,128)S(1)}, u32[]{:S(2)}, u32[]{:S(2)}) collective-permute-start(f32[2,1024]{1,0:T(2,128)S(1)} %add.44), channel_id=1, source_target_pairs={{0,2},{2,0},{1,3},{3,1},{4,6},{6,4},{5,7},{7,5},{8,10},{10,8},{9,1... | collective-permute-start | bytes 24584 | tf_op jit(solution)/shard_map/ppermute | solution.py:450
  224.2 19.4 %collective-permute-start.28 = (f32[2,1024]{1,0:T(2,128)S(1)}, f32[2,1024]{1,0:T(2,128)S(1)}, u32[]{:S(2)}, u32[]{:S(2)}) collective-permute-start(f32[2,1024]{1,0:T(2,128)S(1)} %add.45), channel_id=1, source_target_pairs={{0,4},{4,8},{8,12},{12,0},{1,5},{5,9},{9,13},{13,1},{2,6},{6,10},{... | collective-permute-start | bytes 24584 | tf_op jit(solution)/shard_map/ppermute | solution.py:450
  243.7 4.4 %collective-permute-start.29 = (f32[2,1024]{1,0:T(2,128)S(1)}, f32[2,1024]{1,0:T(2,128)S(1)}, u32[]{:S(2)}, u32[]{:S(2)}) collective-permute-start(f32[2,1024]{1,0:T(2,128)S(1)} %add.46), channel_id=1, source_target_pairs={{0,8},{4,12},{8,0},{12,4},{1,9},{5,13},{9,1},{13,5},{2,10},{6,14},... | collective-permute-start | bytes 24584 | tf_op jit(solution)/shard_map/ppermute | solution.py:450
  248.1 7.2 %collective-permute-start.30 = (f32[2,1024]{1,0:T(2,128)S(1)}, f32[2,1024]{1,0:T(2,128)S(1)}, u32[]{:S(2)}, u32[]{:S(2)}) collective-permute-start(f32[2,1024]{1,0:T(2,128)S(1)} %add.47), channel_id=1, source_target_pairs={{0,16},{16,32},{32,48},{48,0},{1,17},{17,33},{33,49},{49,1},{2,18}... | collective-permute-start | bytes 24584 | tf_op jit(solution)/shard_map/ppermute | solution.py:450
  255.3 2.2 collective-permute-start.38
  256.0 40.3 %collective-permute-start.39 = (bf16[528,512]{1,0:T(8,128)(2,1)}, bf16[528,512]{1,0:T(8,128)(2,1)}, u32[]{:S(2)}, u32[]{:S(2)}) collective-permute-start(bf16[528,512]{1,0:T(8,128)(2,1)} %get-tuple-element.370), channel_id=1, source_target_pairs={{64,76},{65,113},{68,64},{69,117},{72,68},{73,121},{76,72},{77,125... | collective-permute-start | bytes 1622024 | tf_op jit(solution)/shard_map/ppermute | solution.py:465
  257.5 70.0 %collective-permute-start.3 = (bf16[512,1024]{1,0:T(8,128)(2,1)}, bf16[512,1024]{1,0:T(8,128)(2,1)}, u32[]{:S(2)}, u32[]{:S(2)}) collective-permute-start(bf16[512,1024]{1,0:T(8,128)(2,1)} %get-tuple-element.336), channel_id=1, source_target_pairs={{0,64},{1,65},{2,66},{3,67},{4,68},{5,69},{6,70},{7,71},{8,72},{9,... | collective-permute-start | bytes 3145736 | tf_op jit(solution)/shard_map/ppermute | solution.py:454
  296.3 4.2 %collective-permute-start.31 = (f32[2,1024]{1,0:T(2,128)S(1)}, f32[2,1024]{1,0:T(2,128)S(1)}, u32[]{:S(2)}, u32[]{:S(2)}) collective-permute-start(f32[2,1024]{1,0:T(2,128)S(1)} %add.48), channel_id=1, source_target_pairs={{0,32},{16,48},{32,0},{48,16},{1,33},{17,49},{33,1},{49,17},{2,34}... | collective-permute-start | bytes 24584 | tf_op jit(solution)/shard_map/ppermute | solution.py:450
  300.4 21.6 %collective-permute-start.40 = (bf16[3,88,512]{2,1,0:T(8,128)(2,1)S(1)}, bf16[3,88,512]{2,1,0:T(8,128)(2,1)S(1)}, u32[]{:S(2)}, u32[]{:S(2)}) collective-permute-start(bf16[3,88,512]{2,1,0:T(8,128)(2,1)S(1)} %dynamic-slice_bitcast_fusion.1), channel_id=1, source_target_pairs={{0,2},{2,0},{1,3},{3,1},{4,6},{6,4},{5,7},{7,5},{8,10},{10,8},{9,1... | collective-permute-start | bytes 811016 | tf_op jit(solution)/shard_map/ppermute | solution.py:450
  322.0 12.1 %collective-permute-start.22 = (bf16[4,2,4,32,512]{4,3,2,1,0:T(8,128)(2,1)S(1)}, bf16[4,2,4,32,512]{4,3,2,1,0:T(8,128)(2,1)}, u32[]{:S(2)}, u32[]{:S(2)}) collective-permute-start(bf16[4,2,4,32,512]{4,3,2,1,0:T(8,128)(2,1)S(1)} %pad_maximum_fusion.refs_0_), channel_id=1, source_target_pairs={{0,1},{1,0},{2,3},{3,2},{4,5},{5,4},{6,7},{7,6},{8,9},{9,8},{10,11... | collective-permute-start | bytes 3145736 | tf_op jit(solution)/shard_map/ppermute | solution.py:450
  326.0 4.2 %copy-start.4 = (bf16[4,2,4,32,512]{4,3,2,1,0:T(8,128)(2,1)}, bf16[4,2,4,32,512]{4,3,2,1,0:T(8,128)(2,1)S(1)}, u32[]{:S(2)}) copy-start(bf16[4,2,4,32,512]{4,3,2,1,0:T(8,128)(2,1)S(1)} %collective-permute-done.21.refs_3_) | copy-start | bytes 3145732
  326.0 8.1 %collective-permute-start.25 = (bf16[4,2,4,32,512]{4,3,2,1,0:T(8,128)(2,1)S(1)}, bf16[4,2,4,32,512]{4,3,2,1,0:T(8,128)(2,1)}, u32[]{:S(2)}, u32[]{:S(2)}) collective-permute-start(bf16[4,2,4,32,512]{4,3,2,1,0:T(8,128)(2,1)S(1)} %collective-permute-done.21.refs_3_), channel_id=1, source_target_pairs={{0,1},{1,0},{2,3},{3,2},{4,5},{5,4},{6,7},{7,6},{8,9},{9,8},{10,11... | collective-permute-start | bytes 3145736 | tf_op jit(solution)/shard_map/ppermute | solution.py:450
  326.2 8.0 %collective-permute-start.24 = (bf16[4,2,4,32,512]{4,3,2,1,0:T(8,128)(2,1)}, bf16[4,2,4,32,512]{4,3,2,1,0:T(8,128)(2,1)}, u32[]{:S(2)}, u32[]{:S(2)}) collective-permute-start(bf16[4,2,4,32,512]{4,3,2,1,0:T(8,128)(2,1)} %collective-permute-done.20.refs_2_), channel_id=1, source_target_pairs={{0,1},{1,0},{2,3},{3,2},{4,5},{5,4},{6,7},{7,6},{8,9},{9,8},{10,11... | collective-permute-start | bytes 3145736 | tf_op jit(solution)/shard_map/ppermute | solution.py:450
  326.6 7.6 %collective-permute-start.23 = (bf16[4,2,4,32,512]{4,3,2,1,0:T(8,128)(2,1)}, bf16[4,2,4,32,512]{4,3,2,1,0:T(8,128)(2,1)}, u32[]{:S(2)}, u32[]{:S(2)}) collective-permute-start(bf16[4,2,4,32,512]{4,3,2,1,0:T(8,128)(2,1)} %collective-permute-done.19.refs_1_), channel_id=1, source_target_pairs={{0,1},{1,0},{2,3},{3,2},{4,5},{5,4},{6,7},{7,6},{8,9},{9,8},{10,11... | collective-permute-start | bytes 3145736 | tf_op jit(solution)/shard_map/ppermute | solution.py:450
  327.5 4.3 %collective-permute-start.41 = (bf16[3,44,512]{2,1,0:T(8,128)(2,1)S(1)}, bf16[3,44,512]{2,1,0:T(8,128)(2,1)S(1)}, u32[]{:S(2)}, u32[]{:S(2)}) collective-permute-start(bf16[3,44,512]{2,1,0:T(8,128)(2,1)S(1)} %dynamic-slice_bitcast_fusion.3), channel_id=1, source_target_pairs={{0,1},{1,0},{2,3},{3,2},{4,5},{5,4},{6,7},{7,6},{8,9},{9,8},{10,11... | collective-permute-start | bytes 405512 | tf_op jit(solution)/shard_map/ppermute | solution.py:450
